TPU v7x, 32 devices: a whole 2x2x4 slice. The times are simulated.
32 devices in a mesh: band: 4 (over y, x), space: 8 (over z, core).
Axes of the slice: x: 2, y: 2, z: 4, core: 2. Of those that a mesh axis runs over, the one named last changes fastest.
Arguments:
- orbitals: float32 [4, 192, 192, 192], P('band', 'space'), may hold values from -6 to 6
- occupations: int32 [4], replicated, may hold values from 1 to 4
Outputs:
- exchange_potential: float32 [4, 192, 192, 192], P('band', 'space')
All inputs are finite; a program needn't handle non-finite values.
Results may differ from a plain program's by a relative error of at most 0.0003.
Values sent between devices are 32-bit elements; how exact they have to be, the bound alone decides.
A program may use at most 128 MiB of HBM per device.

v0:
```python
import math

import jax
import jax.numpy as jnp
from jax import lax
from jax.sharding import PartitionSpec as P

STEPS = 2


def shifted(array, axis, by):
    length = lax.axis_size(axis)
    return lax.ppermute(array, axis, [(i, (i + by) % length) for i in range(length)])


def hartley_table(length):
    row_index = lax.broadcasted_iota(jnp.int32, (length, length), 0)
    col_index = lax.broadcasted_iota(jnp.int32, (length, length), 1)
    phase = (row_index * col_index % length).astype(jnp.float32) * (2.0 * math.pi / length)
    return jnp.cos(phase) + jnp.sin(phase)


def folded_square(index, length):
    folded = jnp.minimum(index, length - index)
    return folded * folded


def kernel_block(length, first_row, row_count):
    shape = (length, row_count, length)
    squares = folded_square(lax.broadcasted_iota(jnp.int32, shape, 0), length)
    squares = squares + folded_square(first_row + lax.broadcasted_iota(jnp.int32, shape, 1), length)
    squares = squares + folded_square(lax.broadcasted_iota(jnp.int32, shape, 2), length)
    lowest = (2.0 * math.pi / length) ** 2
    values = 1.0 / (lowest * (1.0 + squares.astype(jnp.float32)))
    values = jnp.where(squares > 0, values, jnp.zeros_like(values))
    return values / float(length**3)


def transform_along(field, table, axis_number):
    if axis_number == 1:
        return jnp.einsum("pxyz,kx->pkyz", field, table, precision=lax.Precision.HIGHEST)
    if axis_number == 2:
        return jnp.einsum("pxyz,ky->pxkz", field, table, precision=lax.Precision.HIGHEST)
    return jnp.einsum("pxyz,kz->pxyk", field, table, precision=lax.Precision.HIGHEST)


def potentials(densities, table, kernel):
    spectra = transform_along(transform_along(densities, table, 3), table, 2)
    image = (
        transform_along(
            lax.all_to_all(spectra, "space", split_axis=2, concat_axis=1, tiled=True), table, 1
        )
        * kernel
    )
    solved = transform_along(image, table, 1)
    mixed = lax.all_to_all(solved, "space", split_axis=1, concat_axis=2, tiled=True)
    return transform_along(transform_along(mixed, table, 2), table, 3)


def shards(orbitals, occupations):
    owned_count = orbitals.shape[0]
    slab_rows = orbitals.shape[1]
    length = orbitals.shape[2]
    group_count = lax.axis_size("band")
    own_group = lax.axis_index("band")
    table = hartley_table(length)
    kernel = kernel_block(length, lax.axis_index("space") * slab_rows, slab_rows)
    weight_table = occupations.reshape(group_count, owned_count).astype(jnp.float32)

    def group_weights(offset):
        row_number = (
            own_group - offset + 2 * group_count * (offset // group_count + 1)
        ) % group_count
        return lax.dynamic_index_in_dim(weight_table, row_number, 0, keepdims=False)

    def evaluate(left_fields, right_fields):
        return [
            potentials((left_one * right_one)[None], table, kernel)[0]
            for left_one, right_one in zip(left_fields, right_fields)
        ]

    own_weights = group_weights(0)
    zero_field = jnp.zeros((slab_rows, length, length), jnp.float32)
    pair_list = [
        (left_band, right_band)
        for left_band in range(owned_count)
        for right_band in range(left_band, owned_count)
    ]
    combos = [
        (own_band, guest_band)
        for own_band in range(owned_count)
        for guest_band in range(owned_count)
    ]

    def visit_lists(visitors):
        return (
            [orbitals[own_band] for own_band, _ in combos],
            [visitors[guest_band] for _, guest_band in combos],
        )

    def apply_visit(visitors, offset, solved, partial_value, results):
        guest_weights = group_weights(offset)
        results = list(results)
        partial_list = [partial_value[0]]
        for (own_band, guest_band), field in zip(combos, solved):
            results[own_band] = (
                results[own_band] + guest_weights[guest_band] * visitors[guest_band] * field
            )
            partial_list[guest_band] = (
                partial_list[guest_band] + own_weights[own_band] * orbitals[own_band] * field
            )
        return (jnp.stack(partial_list), results)

    def visit(visitors, offset, partial_value, results):
        left_fields, right_fields = visit_lists(visitors)
        solved = evaluate(left_fields, right_fields)
        return apply_visit(visitors, offset, solved, partial_value, results)

    empty_partial = jnp.zeros(orbitals.shape, jnp.float32)
    empty_results = [zero_field]
    left_fields = [orbitals[left_band] for left_band, _ in pair_list]
    right_fields = [orbitals[right_band] for _, right_band in pair_list]
    solved_list = evaluate(left_fields, right_fields)
    results = empty_results
    results = list(results)
    for (left_band, right_band), field in zip(pair_list, solved_list):
        results[left_band] = own_weights[right_band] * orbitals[right_band] * field
    visitors = shifted(orbitals, "band", 1)
    partial_value, results = visit(visitors, 1, empty_partial, results)
    offset = 2
    visitors, partial_value = shifted((visitors, partial_value), "band", 1)
    partial_value, results = visit(visitors, offset, partial_value, results)
    returned = shifted(partial_value, "band", -STEPS)
    total = jnp.stack(results) + returned
    return -total


def solution(mesh):
    placed = (P("band", "space", None, None), P())
    return jax.shard_map(
        shards,
        mesh=mesh,
        in_specs=placed,
        out_specs=P("band", "space", None, None),
        check_vma=False,
    )
```

profile of v0, /device:TPU:0, one launch (start us, length us, event | category | flops | bytes accessed | tf_op | source)
XLA Modules:
  0.0 757.6 jit_solution(16489586913322929619)
XLA Ops:
  0.0 7.0 fusion.14
  17.2 6.3 all-to-all-start
  25.0 103.8 %collective-permute-done = f32[1,24,192,192]{3,2,1,0:T(8,128)S(1)} collective-permute-done((f32[1,24,192,192]{3,2,1,0:T(8,128)}, f32[1,24,192,192]{3,2,1,0:T(8,128)S(1)}, u32[]{:S(2)}, u32[]{:S(2)}) %collective-permute-start) | collective-permute-done | bytes 3538976 | tf_op jit(solution)/shard_map/ppermute | solution.py:13
  128.8 8.9 %fusion.11 = f32[24,192,192]{2,1,0:T(8,128)S(1)} fusion(f32[1,24,192,192]{3,2,1,0:T(8,128)} %param.2, f32[1,24,192,192]{3,2,1,0:T(8,128)S(1)} %collective-permute-done), kind=kOutput, calls=%fused_computation.14 | convolution fusion | flops 2039685120 | bytes 10616832 | tf_op jit(solution)/shard_map/pxyz,kz->pxyk/dot_general | solution.py:44
  137.7 5.6 convolution_bitcast_fusion.1
  143.3 5.3 copy.30
  154.0 104.7 %collective-permute-done.1 = f32[1,24,192,192]{3,2,1,0:T(8,128)S(1)} collective-permute-done((f32[1,24,192,192]{3,2,1,0:T(8,128)}, f32[1,24,192,192]{3,2,1,0:T(8,128)S(1)}, u32[]{:S(2)}, u32[]{:S(2)}) %collective-permute-start.1) | collective-permute-done | bytes 3538976 | tf_op jit(solution)/shard_map/ppermute | solution.py:13
  260.9 7.2 fusion.8
  287.4 6.4 fusion.19
  293.8 7.0 fusion.36
  305.8 82.6 %all-to-all-done.4 = f32[1,24,192,192]{3,1,0,2:T(8,128)} async-done(((f32[1,24,192,192]{3,1,0,2:T(8,128)}), f32[1,24,192,192]{3,1,0,2:T(8,128)}, u32[]{:S(2)}, u32[]{:S(2)}) %all-to-all-start.4) | async-done | bytes 3538976 | tf_op jit(solution)/shard_map/all_to_all | solution.py:51
  397.3 6.5 fusion.17
  403.8 6.8 fusion.39
  415.5 82.8 %all-to-all-done.3 = f32[1,192,24,192]{3,2,0,1:T(8,128)} async-done(((f32[1,192,24,192]{3,2,0,1:T(8,128)}), f32[1,192,24,192]{3,2,0,1:T(8,128)}, u32[]{:S(2)}, u32[]{:S(2)}) %all-to-all-start.3) | async-done | bytes 3538976 | tf_op jit(solution)/shard_map/all_to_all | solution.py:56
  507.9 6.4 fusion.21
  517.3 5.3 fusion.52
  531.6 6.3 fusion.33
  542.8 65.3 %all-to-all-done.5 = f32[1,192,24,192]{3,2,0,1:T(8,128)} async-done(((f32[1,192,24,192]{3,2,0,1:T(8,128)}), f32[1,192,24,192]{3,2,0,1:T(8,128)}, u32[]{:S(2)}, u32[]{:S(2)}) %all-to-all-start.5) | async-done | bytes 3538976 | tf_op jit(solution)/shard_map/all_to_all | solution.py:56
  625.8 11.1 %collective-permute-done.2 = f32[1,24,192,192]{3,2,1,0:T(8,128)} collective-permute-done((f32[1,24,192,192]{3,2,1,0:T(8,128)}, f32[1,24,192,192]{3,2,1,0:T(8,128)}, u32[]{:S(2)}, u32[]{:S(2)}) %collective-permute-start.2) | collective-permute-done | bytes 3538976 | tf_op jit(solution)/shard_map/ppermute | solution.py:13
  636.9 6.7 fusion.6
  645.1 72.9 %all-to-all-done.1 = f32[1,192,24,192]{3,2,0,1:T(8,128)} async-done(((f32[1,192,24,192]{3,2,0,1:T(8,128)}), f32[1,192,24,192]{3,2,0,1:T(8,128)}, u32[]{:S(2)}, u32[]{:S(2)}) %all-to-all-start.1) | async-done | bytes 3538976 | tf_op jit(solution)/shard_map/all_to_all | solution.py:56
  726.4 6.8 fusion.4
  733.2 13.9 %collective-permute-done.3 = f32[1,24,192,192]{3,2,1,0:T(8,128)} collective-permute-done((f32[1,24,192,192]{3,2,1,0:T(8,128)}, f32[1,24,192,192]{3,2,1,0:T(8,128)}, u32[]{:S(2)}, u32[]{:S(2)}) %collective-permute-start.3) | collective-permute-done | bytes 3538976 | tf_op jit(solution)/shard_map/ppermute | solution.py:13
  747.2 10.1 %fusion.7 = f32[1,24,192,192]{3,2,1,0:T(8,128)} fusion(f32[1,24,192,192]{3,2,1,0:T(8,128)} %collective-permute-done.3, f32[24,192,192]{2,1,0:T(8,128)S(1)} %bitcast.161, f32[24,192,192]{2,1,0:T(8,128)S(1)} %bitcast.159, f32[24,192,192]{2,1,0:T(8,128)} %fusion.4, f32[1,24,192,192]{3,2,1,0:T(8,128)} %copy-done.3, f32[1,24,192,192]{3,2,1,0:T(8,128)S(1)} %bitcast.163, ...), kind=kLoop, calls=%fused_computation.9 | loop fusion | flops 8847360 | bytes 28311564 | tf_op jit(solution)/shard_map/neg | solution.py:135
  (76 shorter events, 111.0 us)
Async XLA Ops:
  17.2 131.5 %all-to-all-start = ((f32[1,24,192,192]{3,1,0,2:T(8,128)}), f32[1,24,192,192]{3,1,0,2:T(8,128)}, u32[]{:S(2)}, u32[]{:S(2)}) async-start(f32[1,24,192,192]{3,1,0,2:T(8,128)} %copy.24), calls=%async_computation | async-start | bytes 9437184 | tf_op jit(solution)/shard_map/all_to_all | solution.py:51
  23.5 105.3 %collective-permute-start = (f32[1,24,192,192]{3,2,1,0:T(8,128)}, f32[1,24,192,192]{3,2,1,0:T(8,128)S(1)}, u32[]{:S(2)}, u32[]{:S(2)}) collective-permute-start(f32[1,24,192,192]{3,2,1,0:T(8,128)} %param.2), channel_id=1, source_target_pairs={{0,8},{8,16},{16,24},{24,0},{1,9},{9,17},{17,25},{25,1},{2,10},{10... | collective-permute-start | bytes 10616840 | tf_op jit(solution)/shard_map/ppermute | solution.py:13
  128.8 8.9 %copy-start.2 = (f32[1,24,192,192]{3,2,1,0:T(8,128)}, f32[1,24,192,192]{3,2,1,0:T(8,128)S(1)}, u32[]{:S(2)}) copy-start(f32[1,24,192,192]{3,2,1,0:T(8,128)S(1)} %collective-permute-done) | copy-start | bytes 10616836
  148.7 129.6 %all-to-all-start.2 = ((f32[1,24,192,192]{3,1,0,2:T(8,128)}), f32[1,24,192,192]{3,1,0,2:T(8,128)}, u32[]{:S(2)}, u32[]{:S(2)}) async-start(f32[1,24,192,192]{3,1,0,2:T(8,128)} %copy.30), calls=%async_computation.2 | async-start | bytes 9437184 | tf_op jit(solution)/shard_map/all_to_all | solution.py:51
  153.4 105.3 %collective-permute-start.1 = (f32[1,24,192,192]{3,2,1,0:T(8,128)}, f32[1,24,192,192]{3,2,1,0:T(8,128)S(1)}, u32[]{:S(2)}, u32[]{:S(2)}) collective-permute-start(f32[1,24,192,192]{3,2,1,0:T(8,128)} %copy-done.2), channel_id=1, source_target_pairs={{0,8},{8,16},{16,24},{24,0},{1,9},{9,17},{17,25},{25,1},{2,10},{10... | collective-permute-start | bytes 10616840 | tf_op jit(solution)/shard_map/ppermute | solution.py:13
  278.3 110.1 %all-to-all-start.4 = ((f32[1,24,192,192]{3,1,0,2:T(8,128)}), f32[1,24,192,192]{3,1,0,2:T(8,128)}, u32[]{:S(2)}, u32[]{:S(2)}) async-start(f32[1,24,192,192]{3,1,0,2:T(8,128)} %copy.36), calls=%async_computation.4 | async-start | bytes 9437184 | tf_op jit(solution)/shard_map/all_to_all | solution.py:51
  388.4 109.8 %all-to-all-start.3 = ((f32[1,192,24,192]{3,2,0,1:T(8,128)}), f32[1,192,24,192]{3,2,0,1:T(8,128)}, u32[]{:S(2)}, u32[]{:S(2)}) async-start(f32[1,192,24,192]{3,2,0,1:T(8,128)} %copy.34), calls=%async_computation.3 | async-start | bytes 9437184 | tf_op jit(solution)/shard_map/all_to_all | solution.py:56
  415.5 87.4 %copy-start.4 = (s32[4]{0:T(128)S(1)}, s32[4]{0:T(128)}, u32[]{:S(2)}) copy-start(s32[4]{0:T(128)} %param.3) | copy-start | bytes 52
  498.3 109.9 %all-to-all-start.5 = ((f32[1,192,24,192]{3,2,0,1:T(8,128)}), f32[1,192,24,192]{3,2,0,1:T(8,128)}, u32[]{:S(2)}, u32[]{:S(2)}) async-start(f32[1,192,24,192]{3,2,0,1:T(8,128)} %copy.40), calls=%async_computation.5 | async-start | bytes 9437184 | tf_op jit(solution)/shard_map/all_to_all | solution.py:56
  517.3 10.3 %slice-start = ((s8[4718592]{0:T(1024)(128)(4,1)}), s8[4194304]{0:T(1024)(128)(4,1)S(1)}, s32[]{:S(2)}) async-start(s8[4718592]{0:T(1024)(128)(4,1)} %bitcast.152), calls=%async_computation.6 | async-start | bytes 8388608
  531.2 105.6 %collective-permute-start.2 = (f32[1,24,192,192]{3,2,1,0:T(8,128)}, f32[1,24,192,192]{3,2,1,0:T(8,128)}, u32[]{:S(2)}, u32[]{:S(2)}) collective-permute-start(f32[1,24,192,192]{3,2,1,0:T(8,128)} %fusion.16), channel_id=1, source_target_pairs={{0,8},{8,16},{16,24},{24,0},{1,9},{9,17},{17,25},{25,1},{2,10},{10... | collective-permute-start | bytes 10616840 | tf_op jit(solution)/shard_map/ppermute | solution.py:13
  608.1 109.9 %all-to-all-start.1 = ((f32[1,192,24,192]{3,2,0,1:T(8,128)}), f32[1,192,24,192]{3,2,0,1:T(8,128)}, u32[]{:S(2)}, u32[]{:S(2)}) async-start(f32[1,192,24,192]{3,2,0,1:T(8,128)} %copy.28), calls=%async_computation.1 | async-start | bytes 9437184 | tf_op jit(solution)/shard_map/all_to_all | solution.py:56
  615.8 21.1 %slice-start.2 = ((s8[4718592]{0:T(1024)(128)(4,1)}), s8[4194304]{0:T(1024)(128)(4,1)S(1)}, s32[]{:S(2)}) async-start(s8[4718592]{0:T(1024)(128)(4,1)} %bitcast.154), calls=%async_computation.8 | async-start | bytes 8388608
  620.9 16.0 %slice-start.3 = ((s8[4718592]{0:T(1024)(128)(4,1)}), s8[524288]{0:T(1024)(128)(4,1)S(1)}, s32[]{:S(2)}) async-start(s8[4718592]{0:T(1024)(128)(4,1)} %bitcast.154), calls=%async_computation.9 | async-start | bytes 1048576
  625.8 17.8 %copy-start.1 = (f32[24,192,192]{2,1,0:T(8,128)}, f32[24,192,192]{2,1,0:T(8,128)S(1)}, u32[]{:S(2)}) copy-start(f32[24,192,192]{2,1,0:T(8,128)S(1)} %fusion) | copy-start | bytes 10616836
  636.9 110.2 %slice-start.10 = ((s8[4718592]{0:T(1024)(128)(4,1)}), s8[524288]{0:T(1024)(128)(4,1)S(1)}, s32[]{:S(2)}) async-start(s8[4718592]{0:T(1024)(128)(4,1)} %bitcast.162), calls=%async_computation.16 | async-start | bytes 1048576
  643.6 103.5 %collective-permute-start.3 = (f32[1,24,192,192]{3,2,1,0:T(8,128)}, f32[1,24,192,192]{3,2,1,0:T(8,128)}, u32[]{:S(2)}, u32[]{:S(2)}) collective-permute-start(f32[1,24,192,192]{3,2,1,0:T(8,128)} %fusion.6), channel_id=1, source_target_pairs={{0,16},{8,24},{16,0},{24,8},{1,17},{9,25},{17,1},{25,9},{2,18},{10... | collective-permute-start | bytes 10616840 | tf_op jit(solution)/shard_map/ppermute | solution.py:13
  718.0 29.2 %slice-start.11 = ((s8[4718592]{0:T(1024)(128)(4,1)}), s8[4194304]{0:T(1024)(128)(4,1)S(1)}, s32[]{:S(2)}) async-start(s8[4718592]{0:T(1024)(128)(4,1)} %bitcast.162), calls=%async_computation.17 | async-start | bytes 8388608
  721.0 26.1 %slice-start.4 = ((s8[4718592]{0:T(1024)(128)(4,1)}), s8[4194304]{0:T(1024)(128)(4,1)S(1)}, s32[]{:S(2)}) async-start(s8[4718592]{0:T(1024)(128)(4,1)} %bitcast.156), calls=%async_computation.10 | async-start | bytes 8388608
  721.1 26.1 %slice-start.6 = ((s8[4718592]{0:T(1024)(128)(4,1)}), s8[4194304]{0:T(1024)(128)(4,1)S(1)}, s32[]{:S(2)}) async-start(s8[4718592]{0:T(1024)(128)(4,1)} %bitcast.158), calls=%async_computation.12 | async-start | bytes 8388608
  721.1 26.1 %slice-start.8 = ((s8[4718592]{0:T(1024)(128)(4,1)}), s8[4194304]{0:T(1024)(128)(4,1)S(1)}, s32[]{:S(2)}) async-start(s8[4718592]{0:T(1024)(128)(4,1)} %bitcast.160), calls=%async_computation.14 | async-start | bytes 8388608
  726.4 20.8 %slice-start.5 = ((s8[4718592]{0:T(1024)(128)(4,1)}), s8[524288]{0:T(1024)(128)(4,1)S(1)}, s32[]{:S(2)}) async-start(s8[4718592]{0:T(1024)(128)(4,1)} %bitcast.156), calls=%async_computation.11 | async-start | bytes 1048576
  726.4 20.8 %slice-start.7 = ((s8[4718592]{0:T(1024)(128)(4,1)}), s8[524288]{0:T(1024)(128)(4,1)S(1)}, s32[]{:S(2)}) async-start(s8[4718592]{0:T(1024)(128)(4,1)} %bitcast.158), calls=%async_computation.13 | async-start | bytes 1048576
  726.4 20.8 %slice-start.9 = ((s8[4718592]{0:T(1024)(128)(4,1)}), s8[524288]{0:T(1024)(128)(4,1)S(1)}, s32[]{:S(2)}) async-start(s8[4718592]{0:T(1024)(128)(4,1)} %bitcast.160), calls=%async_computation.15 | async-start | bytes 1048576
  (3 other events, 10.8 us)
where the time goes:
time: 772 us; the launch traced here: 758 us
  waiting for transfers between devices  537 us (70%)
  matrix products  111 us (14%)
  local copies, waits for them, and re-layouts  54.8 us (7%)
  starting transfers between devices  33.8 us (4%)
  other arithmetic  20.5 us (3%)
    ppermute x4, waiting for transfers between devices, shifted(): lax.ppermute(array, axis, [(i, (i + by) % length) for i in range(length)])  234 us
    all_to_all x3, waiting for transfers between devices, potentials(): lax.all_to_all(solved, 'space', split_axis=1, concat_axis=2, tiled=True)  221 us
    all_to_all x3, waiting for transfers between devices, potentials(): lax.all_to_all(spectra, 'space', split_axis=2, concat_axis=1, tiled=True)  82.6 us
    dot_general x6, matrix products, transform_along(): jnp.einsum('pxyz,kz->pxyk', field, table, precision=lax.Precision.HIGHEST)  39.7 us
    dot_general x6, matrix products, transform_along(): jnp.einsum('pxyz,kx->pkyz', field, table, precision=lax.Precision.HIGHEST)  39.5 us
    dot_general x6, matrix products, transform_along(): jnp.einsum('pxyz,ky->pxkz', field, table, precision=lax.Precision.HIGHEST)  31.5 us
    all_to_all x3, starting transfers between devices, potentials(): lax.all_to_all(spectra, 'space', split_axis=2, concat_axis=1, tiled=True)  15.8 us
    transpose x3, local copies, waits for them, and re-layouts, transform_along(): jnp.einsum('pxyz,ky->pxkz', field, table, precision=lax.Precision.HIGHEST)  15.5 us
  transfers between devices with their start and end apart: 10, of which 8 were waited for; matrix products, arithmetic and copies ran while one was open for 21% of the time, Pallas kernels for 0%

commit v1 on v0

v1 whole, which is shorter than its diff:
```python
import math

import jax
import jax.numpy as jnp
from jax import lax
from jax.sharding import PartitionSpec as P

STEPS = 2
PRECISION = lax.Precision.HIGH


def shifted(array, axis, by):
    length = lax.axis_size(axis)
    return lax.ppermute(array, axis, [(i, (i + by) % length) for i in range(length)])


def shifted_flat(array, axis, by):
    return shifted(array.reshape(-1, 128), axis, by).reshape(array.shape)


def hartley_table(length):
    row_index = lax.broadcasted_iota(jnp.int32, (length, length), 0)
    col_index = lax.broadcasted_iota(jnp.int32, (length, length), 1)
    phase = (row_index * col_index % length).astype(jnp.float32) * (2.0 * math.pi / length)
    return jnp.cos(phase) + jnp.sin(phase)


def folded_square(index, length):
    folded = jnp.minimum(index, length - index)
    return folded * folded


def kernel_block(length, first_row, row_count):
    shape = (length, row_count, length)
    squares = folded_square(lax.broadcasted_iota(jnp.int32, shape, 0), length)
    squares = squares + folded_square(first_row + lax.broadcasted_iota(jnp.int32, shape, 1), length)
    squares = squares + folded_square(lax.broadcasted_iota(jnp.int32, shape, 2), length)
    lowest = (2.0 * math.pi / length) ** 2
    values = 1.0 / (lowest * (1.0 + squares.astype(jnp.float32)))
    values = jnp.where(squares > 0, values, jnp.zeros_like(values))
    return (values / float(length**3)).reshape(length, row_count * length)


def along_z(field, table):
    return jnp.einsum("xyz,kz->xyk", field, table, precision=PRECISION)


def along_y(field, table):
    return jnp.einsum("xyz,ky->xkz", field, table, precision=PRECISION)


def along_x(lines, table):
    return jnp.einsum("xn,kx->kn", lines, table, precision=PRECISION)


def exchange(blocks):
    return lax.all_to_all(blocks, "space", split_axis=0, concat_axis=0, tiled=True)


def to_blocks(spectra):
    space_count = lax.axis_size("space")
    slab_rows, rows, length = spectra.shape
    blocks = spectra.reshape(slab_rows, space_count, rows // space_count * length)
    return blocks.transpose(1, 0, 2)


def from_blocks(blocks, rows):
    slab_rows = blocks.shape[1]
    return blocks.transpose(1, 0, 2).reshape(slab_rows, rows, -1)


def with_level(spectra, level):
    shape = (1,) + spectra.shape[1:]
    row = lax.broadcasted_iota(jnp.int32, shape, 1)
    column = lax.broadcasted_iota(jnp.int32, shape, 2)
    length = spectra.shape[2]
    return spectra + jnp.where((row == 0) & (column == 0), level * float(length**2), 0.0)


def solve_lines(blocks, table, kernel, holds_first):
    count, slab_rows, width = blocks.shape
    lines = blocks.reshape(count * slab_rows, width)
    first = (lax.broadcasted_iota(jnp.int32, (1, width), 1) == 0) & holds_first
    lines = lines - jnp.where(first, jnp.mean(lines[:, :1]), 0.0)
    solved = along_x(along_x(lines, table) * kernel, table)
    return solved.reshape(count, slab_rows, width)


def shards(orbitals, occupations):
    owned = orbitals[0]
    length = owned.shape[1]
    group_count = lax.axis_size("band")
    space_count = lax.axis_size("space")
    own_group = lax.axis_index("band")
    place = lax.axis_index("space")
    row_count = length // space_count
    table = hartley_table(length)
    kernel = kernel_block(length, place * row_count, row_count)
    weights = occupations.astype(jnp.float32)

    def weight(offset):
        return lax.dynamic_index_in_dim(weights, (own_group + offset) % group_count, 0, keepdims=False)

    def forward(density):
        level = jnp.mean(density)
        spectra = along_y(along_z(density - level, table), table)
        return exchange(to_blocks(with_level(spectra, level)))

    def backward(blocks):
        return along_z(along_y(from_blocks(blocks, length), table), table)

    shared = group_count == 2 * STEPS
    solo_offsets = range(1, STEPS if shared else STEPS + 1)
    guests = {offset: shifted_flat(owned, "band", -offset) for offset in range(1, STEPS + 1)}

    sent_self = forward(owned * owned)
    sent = {offset: forward(owned * guests[offset]) for offset in solo_offsets}
    if shared:
        half_rows = length // 2
        half_count = half_rows // space_count
        half = own_group // STEPS
        half_table = lax.dynamic_slice_in_dim(table, half * half_rows, half_rows, 0)
        other_table = lax.dynamic_slice_in_dim(table, (1 - half) * half_rows, half_rows, 0)
        half_kernel = kernel_block(length, half * half_rows + place * half_count, half_count)
        density = owned * guests[STEPS]
        level = jnp.mean(density)
        spectra = along_z(along_y(density - level, half_table), table)
        half_sent = exchange(to_blocks(with_level(spectra, jnp.where(half == 0, level, 0.0))))

    total = jnp.zeros_like(owned)
    returned = jnp.zeros_like(owned)
    for offset in solo_offsets:
        field = backward(exchange(solve_lines(sent[offset], table, kernel, place == 0)))
        total = total + weight(offset) * guests[offset] * field
        returned = returned + shifted_flat(weight(0) * owned * field, "band", offset)
    if shared:
        half_back = exchange(solve_lines(half_sent, table, half_kernel, (place == 0) & (half == 0)))
        other_back = shifted(half_back.reshape(-1, 128), "band", STEPS).reshape(half_back.shape)
        own_part = along_y(along_z(from_blocks(half_back, half_rows), table), half_table.T)
        other_part = along_y(along_z(from_blocks(other_back, half_rows), table), other_table.T)
        total = total + 2.0 * weight(STEPS) * guests[STEPS] * (own_part + other_part)
    field = backward(exchange(solve_lines(sent_self, table, kernel, place == 0)))
    total = total + weight(0) * owned * field
    return -(total + returned)[None]


def solution(mesh):
    placed = (P("band", "space", None, None), P())
    return jax.shard_map(
        shards,
        mesh=mesh,
        in_specs=placed,
        out_specs=P("band", "space", None, None),
        check_vma=False,
    )
```

time: 772 us -> 759 us (0.983)
  waiting for transfers between devices: 537 us -> 422 us
  starting transfers between devices: 33.8 us -> 111 us
  local copies, waits for them, and re-layouts: 54.8 us -> 81.8 us
  matrix products: 111 us -> 96.5 us
  other arithmetic: 20.5 us -> 31.6 us
    ppermute x4, starting transfers between devices: 3.99 us -> 83.5 us  [shifted(): lax.ppermute(array, axis, [(i, (i + by) % length) for i in range(length)])]
    reshape x0 -> x16, local copies, waits for them, and re-layouts: none -> 59.1 us  [the longest x4 20.9 us: shifted_flat(): return shifted(array.reshape(-1, 128), axis, by).reshape(array.shape)]
    ppermute x4, waiting for transfers between devices: 234 us -> 176 us  [shifted(): lax.ppermute(array, axis, [(i, (i + by) % length) for i in range(length)])]
    all_to_all x6, waiting for transfers between devices: 304 us -> 246 us  [exchange(): lax.all_to_all(blocks, 'space', split_axis=0, concat_axis=0, tiled=True)]
    all_to_all x9 -> x0, local copies, waits for them, and re-layouts: 21.9 us -> none  [the longest x6 12.9 us: potentials(): lax.all_to_all(spectra, 'space', split_axis=2, concat_axis=1, tiled=True)]
    transpose x6 -> x4, local copies, waits for them, and re-layouts: 30.1 us -> 13.5 us  [from_blocks(): return blocks.transpose(1, 0, 2).reshape(slab_rows, rows, -1)]
    dot_general x18 -> x20, matrix products: 111 us -> 96.5 us  [the longest x7 38.2 us: along_y(): return jnp.einsum('xyz,ky->xkz', field, table, precision=PRECISION)]
    reduce_sum x0 -> x4, other arithmetic: none -> 12.1 us  [the longest x1 7.37 us: shards(): level = jnp.mean(density)]
  transfers between devices with their start and end apart: 10 -> 10, of which waited for: 8 -> 7; matrix products, arithmetic and copies ran while one was open for 21% -> 20% of each run, Pallas kernels for 0% -> 0%
where the time goes in v1:
time: 759 us; the launch traced here: 749 us
  waiting for transfers between devices  422 us (56%)
  starting transfers between devices  111 us (15%)
  matrix products  96.5 us (13%)
  local copies, waits for them, and re-layouts  81.8 us (11%)
  other arithmetic  31.6 us (4%)
    all_to_all x6, waiting for transfers between devices, exchange(): lax.all_to_all(blocks, 'space', split_axis=0, concat_axis=0, tiled=True)  246 us
    ppermute x4, waiting for transfers between devices, shifted(): lax.ppermute(array, axis, [(i, (i + by) % length) for i in range(length)])  176 us
    ppermute x4, starting transfers between devices, shifted(): lax.ppermute(array, axis, [(i, (i + by) % length) for i in range(length)])  83.5 us
    dot_general x7, matrix products, along_y(): return jnp.einsum('xyz,ky->xkz', field, table, precision=PRECISION)  38.2 us
    dot_general x7, matrix products, along_z(): return jnp.einsum('xyz,kz->xyk', field, table, precision=PRECISION)  31.8 us
    all_to_all x6, starting transfers between devices, exchange(): lax.all_to_all(blocks, 'space', split_axis=0, concat_axis=0, tiled=True)  27.3 us
    dot_general x6, matrix products, along_x(): return jnp.einsum('xn,kx->kn', lines, table, precision=PRECISION)  26.5 us
    reshape x4, local copies, waits for them, and re-layouts, shifted_flat(): return shifted(array.reshape(-1, 128), axis, by).reshape(array.shape)  20.9 us
  transfers between devices with their start and end apart: 10, of which 7 were waited for; matrix products, arithmetic and copies ran while one was open for 20% of the time, Pallas kernels for 0%

profile of v1, /device:TPU:0, one launch (start us, length us, event | category | flops | bytes accessed | tf_op | source)
XLA Modules:
  0.0 749.3 jit_solution(12478580500300588396)
XLA Ops:
  10.4 73.7 %collective-permute-done.1 = f32[6912,128]{1,0:T(8,128)} collective-permute-done((f32[6912,128]{1,0:T(8,128)S(1)}, f32[6912,128]{1,0:T(8,128)}, u32[]{:S(2)}, u32[]{:S(2)}) %collective-permute-start.1) | collective-permute-done | bytes 3538976 | tf_op jit(solution)/shard_map/ppermute | solution.py:14
  94.3 7.4 fusion.26
  102.3 6.8 fusion.11
  118.3 5.3 all-to-all-start.2
  126.3 6.7 fusion.13
  133.0 5.8 add_bitcast_fusion.1
  146.4 19.3 %all-to-all-done.2 = f32[8,24,2304]{2,1,0:T(8,128)} async-done(((f32[8,24,2304]{2,1,0:T(8,128)}), f32[8,24,2304]{2,1,0:T(8,128)}, u32[]{:S(2)}, u32[]{:S(2)}) %all-to-all-start.2) | async-done | bytes 1769504 | tf_op jit(solution)/shard_map/all_to_all | solution.py:57
  171.1 5.3 fusion.9
  176.4 5.8 add_bitcast_fusion
  189.9 60.5 %all-to-all-done = f32[8,24,4608]{2,1,0:T(8,128)} async-done(((f32[8,24,4608]{2,1,0:T(8,128)}), f32[8,24,4608]{2,1,0:T(8,128)}, u32[]{:S(2)}, u32[]{:S(2)}) %all-to-all-start) | async-done | bytes 3538976 | tf_op jit(solution)/shard_map/all_to_all | solution.py:57
  265.1 69.0 %all-to-all-done.4 = f32[8,24,4608]{2,1,0:T(8,128)S(1)} async-done(((f32[8,24,4608]{2,1,0:T(8,128)}), f32[8,24,4608]{2,1,0:T(8,128)S(1)}, u32[]{:S(2)}, u32[]{:S(2)}) %all-to-all-start.4) | async-done | bytes 3538976 | tf_op jit(solution)/shard_map/all_to_all | solution.py:57
  344.2 5.5 convolution_multiply_fusion.1
  354.2 27.3 %all-to-all-done.3 = f32[8,24,2304]{2,1,0:T(8,128)S(1)} async-done(((f32[8,24,2304]{2,1,0:T(8,128)}), f32[8,24,2304]{2,1,0:T(8,128)S(1)}, u32[]{:S(2)}, u32[]{:S(2)}) %all-to-all-start.3) | async-done | bytes 1769504 | tf_op jit(solution)/shard_map/all_to_all | solution.py:57
  386.5 5.5 convolution_multiply_fusion
  396.5 70.0 %all-to-all-done.1 = f32[8,24,4608]{2,1,0:T(8,128)} async-done(((f32[8,24,4608]{2,1,0:T(8,128)}), f32[8,24,4608]{2,1,0:T(8,128)}, u32[]{:S(2)}, u32[]{:S(2)}) %all-to-all-start.1) | async-done | bytes 3538976 | tf_op jit(solution)/shard_map/all_to_all | solution.py:57
  472.0 5.9 copy.29
  477.9 5.5 reshape.175
  483.4 5.7 fusion.48
  489.1 7.2 fusion.15
  496.3 5.7 reshape.188
  502.0 77.5 %collective-permute-start.3 = (f32[6912,128]{1,0:T(8,128)}, f32[6912,128]{1,0:T(8,128)}, u32[]{:S(2)}, u32[]{:S(2)}) collective-permute-start(f32[6912,128]{1,0:T(8,128)} %reshape.188), channel_id=1, source_target_pairs={{0,8},{8,16},{16,24},{24,0},{1,9},{9,17},{17,25},{25,1},{2,10},{10... | collective-permute-start | bytes 10616840 | tf_op jit(solution)/shard_map/ppermute | solution.py:14
  593.7 102.2 %collective-permute-done.2 = f32[3456,128]{1,0:T(8,128)} collective-permute-done((f32[3456,128]{1,0:T(8,128)}, f32[3456,128]{1,0:T(8,128)}, u32[]{:S(2)}, u32[]{:S(2)}) %collective-permute-start.2) | collective-permute-done | bytes 1769504 | tf_op jit(solution)/shard_map/ppermute | solution.py:14
  715.9 5.5 fusion.38
  731.6 17.2 %fusion.6 = f32[1,24,192,192]{3,2,1,0:T(8,128)} fusion(f32[24,192,192]{2,1,0:T(8,128)} %reshape.189, f32[24,192,192]{2,1,0:T(8,128)} %fusion, f32[192,24,192]{2,0,1:T(8,128)} %fusion.58, f32[192,24,192]{2,0,1:T(8,128)} %fusion.55, f32[24,192,192]{2,1,0:T(8,128)} %reshape.176, f32[24,192,192]{2,1,0:T(8,128)} %get-tuple-element.14, ...), kind=kLoop, calls=%fused_computation.9 | loop fusion | flops 9732096 | bytes 31850508 | tf_op jit(solution)/shard_map/neg | solution.py:144
  (81 shorter events, 136.4 us)
Async XLA Ops:
  4.5 79.7 %collective-permute-start.1 = (f32[6912,128]{1,0:T(8,128)S(1)}, f32[6912,128]{1,0:T(8,128)}, u32[]{:S(2)}, u32[]{:S(2)}) collective-permute-start(f32[6912,128]{1,0:T(8,128)S(1)} %reshape_squeeze.4), channel_id=1, source_target_pairs={{0,16},{8,24},{16,0},{24,8},{1,17},{9,25},{17,1},{25,9},{2,18},{10... | collective-permute-start | bytes 10616840 | tf_op jit(solution)/shard_map/ppermute | solution.py:14
  7.5 81.7 %collective-permute-start = (f32[6912,128]{1,0:T(8,128)S(1)}, f32[6912,128]{1,0:T(8,128)}, u32[]{:S(2)}, u32[]{:S(2)}) collective-permute-start(f32[6912,128]{1,0:T(8,128)S(1)} %reshape_squeeze.4), channel_id=1, source_target_pairs={{0,24},{8,0},{16,8},{24,16},{1,25},{9,1},{17,9},{25,17},{2,26},{10... | collective-permute-start | bytes 10616840 | tf_op jit(solution)/shard_map/ppermute | solution.py:14
  94.3 8.0 %copy-start.1 = (f32[192,192]{1,0:T(8,128)S(1)}, f32[192,192]{1,0:T(8,128)}, u32[]{:S(2)}) copy-start(f32[192,192]{1,0:T(8,128)} %sine_add_fusion) | copy-start | bytes 442372
  118.3 47.4 %all-to-all-start.2 = ((f32[8,24,2304]{2,1,0:T(8,128)}), f32[8,24,2304]{2,1,0:T(8,128)}, u32[]{:S(2)}, u32[]{:S(2)}) async-start(f32[8,24,2304]{2,1,0:T(8,128)} %bitcast.123), calls=%async_computation.2 | async-start | bytes 3538944 | tf_op jit(solution)/shard_map/all_to_all | solution.py:57
  165.7 84.7 %all-to-all-start = ((f32[8,24,4608]{2,1,0:T(8,128)}), f32[8,24,4608]{2,1,0:T(8,128)}, u32[]{:S(2)}, u32[]{:S(2)}) async-start(f32[8,24,4608]{2,1,0:T(8,128)} %bitcast.122), calls=%async_computation | async-start | bytes 7077888 | tf_op jit(solution)/shard_map/all_to_all | solution.py:57
  171.0 5.4 copy-start.3
  250.4 83.8 %all-to-all-start.4 = ((f32[8,24,4608]{2,1,0:T(8,128)}), f32[8,24,4608]{2,1,0:T(8,128)S(1)}, u32[]{:S(2)}, u32[]{:S(2)}) async-start(f32[8,24,4608]{2,1,0:T(8,128)} %bitcast.121), calls=%async_computation.4 | async-start | bytes 7077888 | tf_op jit(solution)/shard_map/all_to_all | solution.py:57
  254.3 0.6 copy-start.4
  262.2 77.3 %copy-start.5 = (s32[192]{0:T(256)S(1)}, s32[192]{0:T(256)}, u32[]{:S(2)}) copy-start(s32[192]{0:T(256)} %copy-done.4) | copy-start | bytes 2308
  334.2 1.8 copy-start
  336.0 45.6 %all-to-all-start.3 = ((f32[8,24,2304]{2,1,0:T(8,128)}), f32[8,24,2304]{2,1,0:T(8,128)S(1)}, u32[]{:S(2)}, u32[]{:S(2)}) async-start(f32[8,24,2304]{2,1,0:T(8,128)} %bitcast.129), calls=%async_computation.3 | async-start | bytes 3538944 | tf_op jit(solution)/shard_map/all_to_all | solution.py:57
  381.5 85.0 %all-to-all-start.1 = ((f32[8,24,4608]{2,1,0:T(8,128)}), f32[8,24,4608]{2,1,0:T(8,128)}, u32[]{:S(2)}, u32[]{:S(2)}) async-start(f32[8,24,4608]{2,1,0:T(8,128)} %bitcast.128), calls=%async_computation.1 | async-start | bytes 7077888 | tf_op jit(solution)/shard_map/all_to_all | solution.py:57
  466.5 4.8 copy-start.6
  466.5 241.7 %all-to-all-start.5 = ((f32[8,24,4608]{2,1,0:T(8,128)}), f32[8,24,4608]{2,1,0:T(8,128)}, u32[]{:S(2)}, u32[]{:S(2)}) async-start(f32[8,24,4608]{2,1,0:T(8,128)} %bitcast.127), calls=%async_computation.5 | async-start | bytes 7077888 | tf_op jit(solution)/shard_map/all_to_all | solution.py:57
  477.9 11.2 %slice-start = ((s8[4718592]{0:T(1024)(128)(4,1)}), s8[524288]{0:T(1024)(128)(4,1)S(1)}, s32[]{:S(2)}) async-start(s8[4718592]{0:T(1024)(128)(4,1)} %bitcast.124), calls=%async_computation.6 | async-start | bytes 1048576
  483.4 5.7 slice-start.1
  502.0 224.5 %collective-permute-start.3 = (f32[6912,128]{1,0:T(8,128)}, f32[6912,128]{1,0:T(8,128)}, u32[]{:S(2)}, u32[]{:S(2)}) collective-permute-start(f32[6912,128]{1,0:T(8,128)} %reshape.188), channel_id=1, source_target_pairs={{0,8},{8,16},{16,24},{24,0},{1,9},{9,17},{17,25},{25,1},{2,10},{10... | collective-permute-start | bytes 10616840 | tf_op jit(solution)/shard_map/ppermute | solution.py:14
  580.9 115.0 %collective-permute-start.2 = (f32[3456,128]{1,0:T(8,128)}, f32[3456,128]{1,0:T(8,128)}, u32[]{:S(2)}, u32[]{:S(2)}) collective-permute-start(f32[3456,128]{1,0:T(8,128)} %reshape.181), channel_id=1, source_target_pairs={{0,16},{8,24},{16,0},{24,8},{1,17},{9,25},{17,1},{25,9},{2,18},{10... | collective-permute-start | bytes 5308424 | tf_op jit(solution)/shard_map/ppermute | solution.py:14
  584.8 4.5 copy-start.2

commit v2 on v1

--- a/solution.py
+++ b/solution.py
@@ -9,13 +9,13 @@
 PRECISION = lax.Precision.HIGH
 
 
-def shifted(array, axis, by):
-    length = lax.axis_size(axis)
-    return lax.ppermute(array, axis, [(i, (i + by) % length) for i in range(length)])
+def moved(array, axis, targets):
+    flat = lax.ppermute(array.reshape(-1, 128), axis, list(enumerate(targets)))
+    return flat.reshape(array.shape)
 
 
-def shifted_flat(array, axis, by):
-    return shifted(array.reshape(-1, 128), axis, by).reshape(array.shape)
+def after(array, *earlier):
+    return lax.optimization_barrier((array,) + earlier)[0]
 
 
 def hartley_table(length):
@@ -98,50 +98,86 @@
     kernel = kernel_block(length, place * row_count, row_count)
     weights = occupations.astype(jnp.float32)
 
-    def weight(offset):
-        return lax.dynamic_index_in_dim(weights, (own_group + offset) % group_count, 0, keepdims=False)
+    def pick(values):
+        return jnp.asarray(values)[own_group]
+
+    def weight(groups):
+        return weights[pick(groups)]
+
+    def multiplicity(groups):
+        counts = [
+            sum((j - i - s) % group_count == 0 for s in range(-STEPS, STEPS + 1))
+            for i, j in enumerate(groups)
+        ]
+        return pick(jnp.asarray(counts, jnp.float32))
 
     def forward(density):
         level = jnp.mean(density)
         spectra = along_y(along_z(density - level, table), table)
-        return exchange(to_blocks(with_level(spectra, level)))
+        return to_blocks(with_level(spectra, level))
 
     def backward(blocks):
         return along_z(along_y(from_blocks(blocks, length), table), table)
 
-    shared = group_count == 2 * STEPS
-    solo_offsets = range(1, STEPS if shared else STEPS + 1)
-    guests = {offset: shifted_flat(owned, "band", -offset) for offset in range(1, STEPS + 1)}
+    shared = group_count == 2 * STEPS == 4
+    if shared:
+        ring = [0, 1, 3, 2]
+        solo = [[ring[(ring.index(g) + 1) % 4] for g in range(4)]]
+        opposite = [ring[(ring.index(g) + 2) % 4] for g in range(4)]
+    else:
+        solo = [[(g + s) % group_count for g in range(group_count)] for s in range(1, STEPS + 1)]
 
-    sent_self = forward(owned * owned)
-    sent = {offset: forward(owned * guests[offset]) for offset in solo_offsets}
+    def inverse(groups):
+        return [groups.index(g) for g in range(group_count)]
+
+    groups = list(range(group_count))
+    guests = []
+    source = owned
+    for partners in solo:
+        guests.append(moved(source, "band", inverse(partners)))
+        source = after(owned, guests[-1])
+    if shared:
+        far_guest = moved(source, "band", opposite)
+
+    arrived = exchange(forward(owned * owned))
+    lines_self = arrived
+    solo_lines = []
+    for guest in guests:
+        arrived = exchange(after(forward(owned * guest), arrived))
+        solo_lines.append(arrived)
     if shared:
         half_rows = length // 2
         half_count = half_rows // space_count
-        half = own_group // STEPS
+        half = own_group // 2
         half_table = lax.dynamic_slice_in_dim(table, half * half_rows, half_rows, 0)
         other_table = lax.dynamic_slice_in_dim(table, (1 - half) * half_rows, half_rows, 0)
         half_kernel = kernel_block(length, half * half_rows + place * half_count, half_count)
-        density = owned * guests[STEPS]
+        density = owned * far_guest
         level = jnp.mean(density)
         spectra = along_z(along_y(density - level, half_table), table)
-        half_sent = exchange(to_blocks(with_level(spectra, jnp.where(half == 0, level, 0.0))))
+        blocks = to_blocks(with_level(spectra, jnp.where(half == 0, level, 0.0)))
+        arrived = exchange(after(blocks, arrived))
+        half_lines = arrived
 
     total = jnp.zeros_like(owned)
-    returned = jnp.zeros_like(owned)
-    for offset in solo_offsets:
-        field = backward(exchange(solve_lines(sent[offset], table, kernel, place == 0)))
-        total = total + weight(offset) * guests[offset] * field
-        returned = returned + shifted_flat(weight(0) * owned * field, "band", offset)
+    for partners, guest, lines in zip(solo, guests, solo_lines):
+        solved = solve_lines(lines, table, kernel, place == 0)
+        arrived = exchange(after(solved, arrived))
+        field = multiplicity(partners) * backward(arrived)
+        total = total + weight(partners) * guest * field
+        total = total + moved(weight(groups) * owned * field, "band", partners)
     if shared:
-        half_back = exchange(solve_lines(half_sent, table, half_kernel, (place == 0) & (half == 0)))
-        other_back = shifted(half_back.reshape(-1, 128), "band", STEPS).reshape(half_back.shape)
+        solved = solve_lines(half_lines, table, half_kernel, (place == 0) & (half == 0))
+        arrived = exchange(after(solved, arrived))
+        half_back = arrived
+        other_back = moved(half_back, "band", opposite)
         own_part = along_y(along_z(from_blocks(half_back, half_rows), table), half_table.T)
         other_part = along_y(along_z(from_blocks(other_back, half_rows), table), other_table.T)
-        total = total + 2.0 * weight(STEPS) * guests[STEPS] * (own_part + other_part)
-    field = backward(exchange(solve_lines(sent_self, table, kernel, place == 0)))
-    total = total + weight(0) * owned * field
-    return -(total + returned)[None]
+        scale = multiplicity(opposite) * weight(opposite)
+        total = total + scale * far_guest * (own_part + other_part)
+    solved = solve_lines(lines_self, table, kernel, place == 0)
+    field = backward(exchange(after(solved, arrived)))
+    return -(total + weight(groups) * owned * field)[None]
 
 
 def solution(mesh):

time: 759 us -> 770 us (1.014)
  waiting for transfers between devices: 422 us -> 504 us
  starting transfers between devices: 111 us -> 34.8 us
    ppermute x4, waiting for transfers between devices: 176 us -> 251 us  [moved(): flat = lax.ppermute(array.reshape(-1, 128), axis, list(enumerate(targets)))]
    ppermute x4, starting transfers between devices: 83.5 us -> 8.8 us  [moved(): flat = lax.ppermute(array.reshape(-1, 128), axis, list(enumerate(targets)))]
    reshape x6 -> x7, local copies, waits for them, and re-layouts: 23.9 us -> 25.6 us  [the longest x3 12.9 us: moved(): flat = lax.ppermute(array.reshape(-1, 128), axis, list(enumerate(targets)))]
  transfers between devices with their start and end apart: 10 -> 10, of which waited for: 7 -> 9; matrix products, arithmetic and copies ran while one was open for 20% -> 17% of each run, Pallas kernels for 0% -> 0%
where the time goes in v2:
time: 770 us; the launch traced here: 759 us
  waiting for transfers between devices  504 us (65%)
  matrix products  93.8 us (12%)
  local copies, waits for them, and re-layouts  87.8 us (11%)
  starting transfers between devices  34.8 us (5%)
  other arithmetic  28.7 us (4%)
  between operations  9.92 us (1%)
    all_to_all x6, waiting for transfers between devices, exchange(): lax.all_to_all(blocks, 'space', split_axis=0, concat_axis=0, tiled=True)  253 us
    ppermute x4, waiting for transfers between devices, moved(): flat = lax.ppermute(array.reshape(-1, 128), axis, list(enumerate(targets)))  251 us
    dot_general x7, matrix products, along_y(): return jnp.einsum('xyz,ky->xkz', field, table, precision=PRECISION)  36.8 us
    dot_general x7, matrix products, along_z(): return jnp.einsum('xyz,kz->xyk', field, table, precision=PRECISION)  30.6 us
    dot_general x6, matrix products, along_x(): return jnp.einsum('xn,kx->kn', lines, table, precision=PRECISION)  26.4 us
    all_to_all x6, starting transfers between devices, exchange(): lax.all_to_all(blocks, 'space', split_axis=0, concat_axis=0, tiled=True)  26 us
    reshape x6, local copies, waits for them, and re-layouts, to_blocks(): spectra.reshape(slab_rows, space_count, rows // space_count * length)  20.8 us
  transfers between devices with their start and end apart: 10, of which 9 were waited for; matrix products, arithmetic and copies ran while one was open for 17% of the time, Pallas kernels for 0%

profile of v2, /device:TPU:0, one launch (start us, length us, event | category | flops | bytes accessed | tf_op | source)
XLA Modules:
  0.0 758.9 jit_solution(1412262615850810620)
XLA Ops:
  0.0 5.7 reshape_squeeze.3
  8.7 76.7 %collective-permute-done = f32[6912,128]{1,0:T(8,128)S(1)} collective-permute-done((f32[6912,128]{1,0:T(8,128)}, f32[6912,128]{1,0:T(8,128)S(1)}, u32[]{:S(2)}, u32[]{:S(2)}) %collective-permute-start) | collective-permute-done | bytes 3538976 | tf_op jit(solution)/shard_map/ppermute | solution.py:13
  88.4 5.7 reshape.178
  96.8 76.1 %collective-permute-done.1 = f32[6912,128]{1,0:T(8,128)S(1)} collective-permute-done((f32[6912,128]{1,0:T(8,128)}, f32[6912,128]{1,0:T(8,128)S(1)}, u32[]{:S(2)}, u32[]{:S(2)}) %collective-permute-start.1) | collective-permute-done | bytes 3538976 | tf_op jit(solution)/shard_map/ppermute | solution.py:13
  176.0 7.4 fusion.91
  191.5 5.7 add_bitcast_fusion
  210.7 6.8 fusion.12
  217.5 5.7 add_bitcast_fusion.1
  230.9 59.3 %all-to-all-done = f32[8,24,4608]{2,1,0:T(8,128)} async-done(((f32[8,24,4608]{2,1,0:T(8,128)}), f32[8,24,4608]{2,1,0:T(8,128)}, u32[]{:S(2)}, u32[]{:S(2)}) %all-to-all-start) | async-done | bytes 3538976 | tf_op jit(solution)/shard_map/all_to_all | solution.py:57
  308.9 65.7 %all-to-all-done.1 = f32[8,24,4608]{2,1,0:T(8,128)} async-done(((f32[8,24,4608]{2,1,0:T(8,128)}), f32[8,24,4608]{2,1,0:T(8,128)}, u32[]{:S(2)}, u32[]{:S(2)}) %all-to-all-start.1) | async-done | bytes 3538976 | tf_op jit(solution)/shard_map/all_to_all | solution.py:57
  383.4 5.5 convolution_multiply_fusion.1
  393.3 27.0 %all-to-all-done.2 = f32[8,24,2304]{2,1,0:T(8,128)S(1)} async-done(((f32[8,24,2304]{2,1,0:T(8,128)}), f32[8,24,2304]{2,1,0:T(8,128)S(1)}, u32[]{:S(2)}, u32[]{:S(2)}) %all-to-all-start.2) | async-done | bytes 1769504 | tf_op jit(solution)/shard_map/all_to_all | solution.py:57
  436.0 69.1 %all-to-all-done.3 = f32[8,24,4608]{2,1,0:T(8,128)S(1)} async-done(((f32[8,24,4608]{2,1,0:T(8,128)}), f32[8,24,4608]{2,1,0:T(8,128)S(1)}, u32[]{:S(2)}, u32[]{:S(2)}) %all-to-all-start.3) | async-done | bytes 3538976 | tf_op jit(solution)/shard_map/all_to_all | solution.py:57
  510.7 5.5 convolution_multiply_fusion
  520.7 31.9 %all-to-all-done.4 = f32[8,24,2304]{2,1,0:T(8,128)S(1)} async-done(((f32[8,24,2304]{2,1,0:T(8,128)}), f32[8,24,2304]{2,1,0:T(8,128)S(1)}, u32[]{:S(2)}, u32[]{:S(2)}) %all-to-all-start.4) | async-done | bytes 1769504 | tf_op jit(solution)/shard_map/all_to_all | solution.py:57
  564.4 5.8 copy.37
  570.2 5.4 reshape.181
  575.6 5.7 fusion.41
  581.3 7.7 %multiply_multiply_fusion = (f32[24,192,192]{2,1,0:T(8,128)}, f32[24,192,192]{2,1,0:T(8,128)}) fusion(f32[]{:T(128)} %bitcast.16, f32[]{:T(128)} %bitcast.2, f32[1,24,192,192]{3,2,1,0:T(8,128)S(1)} %bitcast.123, f32[192,24,192]{2,0,1:T(8,128)S(1)} %fusion.41), kind=kOutput, calls=%fused_computation.19 | convolution fusion | flops 1022238720 | bytes 14155784 | tf_op jit(solution)/shard_map/xyz,kz->xyk/dot_general | solution.py:45
  589.0 5.8 reshape.182
  609.9 64.3 %collective-permute-done.2 = f32[6912,128]{1,0:T(8,128)} collective-permute-done((f32[6912,128]{1,0:T(8,128)}, f32[6912,128]{1,0:T(8,128)}, u32[]{:S(2)}, u32[]{:S(2)}) %collective-permute-start.2) | collective-permute-done | bytes 3538976 | tf_op jit(solution)/shard_map/ppermute | solution.py:13
  679.3 33.8 %collective-permute-done.3 = f32[3456,128]{1,0:T(8,128)} collective-permute-done((f32[3456,128]{1,0:T(8,128)}, f32[3456,128]{1,0:T(8,128)}, u32[]{:S(2)}, u32[]{:S(2)}) %collective-permute-start.3) | collective-permute-done | bytes 1769504 | tf_op jit(solution)/shard_map/ppermute | solution.py:13
  733.1 5.7 fusion.34
  744.0 14.5 %fusion.5 = f32[1,24,192,192]{3,2,1,0:T(8,128)} fusion(f32[24,192,192]{2,1,0:T(8,128)} %fusion, f32[192,24,192]{2,0,1:T(8,128)} %fusion.53, f32[192,24,192]{2,0,1:T(8,128)} %fusion.51, f32[24,192,192]{2,1,0:T(8,128)S(1)} %bitcast.127, f32[24,192,192]{2,1,0:T(8,128)} %reshape.183, f32[24,192,192]{2,1,0:T(8,128)S(1)} %bitcast.129, ...), kind=kLoop, calls=%fused_computation.8 | loop fusion | flops 10616832 | bytes 31850512 | tf_op jit(solution)/shard_map/neg | solution.py:180
  (112 shorter events, 146.7 us)
Async XLA Ops:
  5.7 79.7 %collective-permute-start = (f32[6912,128]{1,0:T(8,128)}, f32[6912,128]{1,0:T(8,128)S(1)}, u32[]{:S(2)}, u32[]{:S(2)}) collective-permute-start(f32[6912,128]{1,0:T(8,128)} %reshape_squeeze.3), channel_id=1, source_target_pairs={{0,16},{8,0},{16,24},{24,8},{1,17},{9,1},{17,25},{25,9},{2,18},{10... | collective-permute-start | bytes 10616840 | tf_op jit(solution)/shard_map/ppermute | solution.py:13
  94.1 78.8 %collective-permute-start.1 = (f32[6912,128]{1,0:T(8,128)}, f32[6912,128]{1,0:T(8,128)S(1)}, u32[]{:S(2)}, u32[]{:S(2)}) collective-permute-start(f32[6912,128]{1,0:T(8,128)} %reshape.178), channel_id=1, source_target_pairs={{0,24},{8,16},{16,8},{24,0},{1,25},{9,17},{17,9},{25,1},{2,26},{10... | collective-permute-start | bytes 10616840 | tf_op jit(solution)/shard_map/ppermute | solution.py:13
  204.9 85.2 %all-to-all-start = ((f32[8,24,4608]{2,1,0:T(8,128)}), f32[8,24,4608]{2,1,0:T(8,128)}, u32[]{:S(2)}, u32[]{:S(2)}) async-start(f32[8,24,4608]{2,1,0:T(8,128)} %bitcast.118), calls=%async_computation | async-start | bytes 7077888 | tf_op jit(solution)/shard_map/all_to_all | solution.py:57
  210.7 6.8 copy-start.4
  290.1 84.5 %all-to-all-start.1 = ((f32[8,24,4608]{2,1,0:T(8,128)}), f32[8,24,4608]{2,1,0:T(8,128)}, u32[]{:S(2)}, u32[]{:S(2)}) async-start(f32[8,24,4608]{2,1,0:T(8,128)} %bitcast.119), calls=%async_computation.1 | async-start | bytes 7077888 | tf_op jit(solution)/shard_map/all_to_all | solution.py:57
  374.6 45.7 %all-to-all-start.2 = ((f32[8,24,2304]{2,1,0:T(8,128)}), f32[8,24,2304]{2,1,0:T(8,128)S(1)}, u32[]{:S(2)}, u32[]{:S(2)}) async-start(f32[8,24,2304]{2,1,0:T(8,128)} %bitcast.120), calls=%async_computation.2 | async-start | bytes 3538944 | tf_op jit(solution)/shard_map/all_to_all | solution.py:57
  378.4 10.5 %copy-start.7 = (s32[192]{0:T(256)}, s32[192]{0:T(256)S(1)}, u32[]{:S(2)}) copy-start(s32[192]{0:T(256)S(1)} %fusion.67) | copy-start | bytes 2308
  378.5 10.4 %copy-start.5 = (s32[4608]{0:T(1024)}, s32[4608]{0:T(1024)S(1)}, u32[]{:S(2)}) copy-start(s32[4608]{0:T(1024)S(1)} %mul.243) | copy-start | bytes 55300
  378.6 10.2 %copy-start.6 = (s32[4608]{0:T(1024)}, s32[4608]{0:T(1024)S(1)}, u32[]{:S(2)}) copy-start(s32[4608]{0:T(1024)S(1)} %mul.242) | copy-start | bytes 55300
  421.6 83.6 %all-to-all-start.3 = ((f32[8,24,4608]{2,1,0:T(8,128)}), f32[8,24,4608]{2,1,0:T(8,128)S(1)}, u32[]{:S(2)}, u32[]{:S(2)}) async-start(f32[8,24,4608]{2,1,0:T(8,128)} %bitcast.133), calls=%async_computation.3 | async-start | bytes 7077888 | tf_op jit(solution)/shard_map/all_to_all | solution.py:57
  433.2 77.5 %copy-start.8 = (s32[192]{0:T(256)S(1)}, s32[192]{0:T(256)}, u32[]{:S(2)}) copy-start(s32[192]{0:T(256)} %copy-done.7) | copy-start | bytes 2308
  506.9 45.8 %all-to-all-start.4 = ((f32[8,24,2304]{2,1,0:T(8,128)}), f32[8,24,2304]{2,1,0:T(8,128)S(1)}, u32[]{:S(2)}, u32[]{:S(2)}) async-start(f32[8,24,2304]{2,1,0:T(8,128)} %bitcast.134), calls=%async_computation.4 | async-start | bytes 3538944 | tf_op jit(solution)/shard_map/all_to_all | solution.py:57
  552.6 5.1 copy-start.12
  552.6 7.2 copy-start.11
  552.6 9.1 %copy-start.9 = (s32[4]{0:T(128)S(1)}, s32[4]{0:T(128)}, u32[]{:S(2)}) copy-start(s32[4]{0:T(128)} %param.9) | copy-start | bytes 52
  552.6 9.1 %copy-start.10 = (f32[4]{0:T(128)S(1)}, f32[4]{0:T(128)}, u32[]{:S(2)}) copy-start(f32[4]{0:T(128)} %constant.93.clone) | copy-start | bytes 52
  552.6 172.8 %all-to-all-start.5 = ((f32[8,24,4608]{2,1,0:T(8,128)}), f32[8,24,4608]{2,1,0:T(8,128)}, u32[]{:S(2)}, u32[]{:S(2)}) async-start(f32[8,24,4608]{2,1,0:T(8,128)} %bitcast.131), calls=%async_computation.5 | async-start | bytes 7077888 | tf_op jit(solution)/shard_map/all_to_all | solution.py:57
  570.2 11.1 %slice-start = ((s8[4718592]{0:T(1024)(128)(4,1)}), s8[524288]{0:T(1024)(128)(4,1)S(1)}, s32[]{:S(2)}) async-start(s8[4718592]{0:T(1024)(128)(4,1)} %bitcast.122), calls=%async_computation.6 | async-start | bytes 1048576
  575.6 5.7 slice-start.1
  594.8 79.3 %collective-permute-start.2 = (f32[6912,128]{1,0:T(8,128)}, f32[6912,128]{1,0:T(8,128)}, u32[]{:S(2)}, u32[]{:S(2)}) collective-permute-start(f32[6912,128]{1,0:T(8,128)} %reshape.182), channel_id=1, source_target_pairs={{0,8},{8,24},{16,0},{24,16},{1,9},{9,25},{17,1},{25,17},{2,10},{10... | collective-permute-start | bytes 10616840 | tf_op jit(solution)/shard_map/ppermute | solution.py:13
  597.8 115.2 %collective-permute-start.3 = (f32[3456,128]{1,0:T(8,128)}, f32[3456,128]{1,0:T(8,128)}, u32[]{:S(2)}, u32[]{:S(2)}) collective-permute-start(f32[3456,128]{1,0:T(8,128)} %reshape.187), channel_id=1, source_target_pairs={{0,24},{8,16},{16,8},{24,0},{1,25},{9,17},{17,9},{25,1},{2,26},{10... | collective-permute-start | bytes 5308424 | tf_op jit(solution)/shard_map/ppermute | solution.py:13
  733.1 10.8 %slice-start.2 = ((s8[4718592]{0:T(1024)(128)(4,1)}), s8[4194304]{0:T(1024)(128)(4,1)S(1)}, s32[]{:S(2)}) async-start(s8[4718592]{0:T(1024)(128)(4,1)} %bitcast.124), calls=%async_computation.8 | async-start | bytes 8388608
  733.1 10.8 %slice-start.4 = ((s8[4718592]{0:T(1024)(128)(4,1)}), s8[4194304]{0:T(1024)(128)(4,1)S(1)}, s32[]{:S(2)}) async-start(s8[4718592]{0:T(1024)(128)(4,1)} %bitcast.126), calls=%async_computation.10 | async-start | bytes 8388608
  733.1 10.8 %slice-start.6 = ((s8[4718592]{0:T(1024)(128)(4,1)}), s8[4194304]{0:T(1024)(128)(4,1)S(1)}, s32[]{:S(2)}) async-start(s8[4718592]{0:T(1024)(128)(4,1)} %bitcast.128), calls=%async_computation.12 | async-start | bytes 8388608
  (7 other events, 23.4 us)

commit v3 on v2

--- a/solution.py
+++ b/solution.py
@@ -9,9 +9,12 @@
 PRECISION = lax.Precision.HIGH
 
 
-def moved(array, axis, targets):
-    flat = lax.ppermute(array.reshape(-1, 128), axis, list(enumerate(targets)))
-    return flat.reshape(array.shape)
+def moved(flat, axis, targets):
+    return lax.ppermute(flat, axis, list(enumerate(targets)))
+
+
+def flattened(array):
+    return array.reshape(-1, 128)
 
 
 def after(array, *earlier):
@@ -131,19 +134,21 @@
         return [groups.index(g) for g in range(group_count)]
 
     groups = list(range(group_count))
+    flat_guests = []
+    source = flattened(owned)
+    for partners in solo + ([opposite] if shared else []):
+        flat_guests.append(moved(source, "band", inverse(partners)))
+        source = after(source, flat_guests[-1])
+
+    blocks = forward(owned * owned)
+    arrived = exchange(blocks)
+    lines_self = arrived
     guests = []
-    source = owned
-    for partners in solo:
-        guests.append(moved(source, "band", inverse(partners)))
-        source = after(owned, guests[-1])
-    if shared:
-        far_guest = moved(source, "band", opposite)
-
-    arrived = exchange(forward(owned * owned))
-    lines_self = arrived
     solo_lines = []
-    for guest in guests:
-        arrived = exchange(after(forward(owned * guest), arrived))
+    for index in range(len(solo)):
+        guests.append(after(flat_guests[index], blocks).reshape(owned.shape))
+        blocks = after(forward(owned * guests[index]), arrived)
+        arrived = exchange(blocks)
         solo_lines.append(arrived)
     if shared:
         half_rows = length // 2
@@ -152,6 +157,7 @@
         half_table = lax.dynamic_slice_in_dim(table, half * half_rows, half_rows, 0)
         other_table = lax.dynamic_slice_in_dim(table, (1 - half) * half_rows, half_rows, 0)
         half_kernel = kernel_block(length, half * half_rows + place * half_count, half_count)
+        far_guest = after(flat_guests[-1], blocks).reshape(owned.shape)
         density = owned * far_guest
         level = jnp.mean(density)
         spectra = along_z(along_y(density - level, half_table), table)
@@ -160,23 +166,31 @@
         half_lines = arrived
 
     total = jnp.zeros_like(owned)
+    partials = []
+    returned = []
     for partners, guest, lines in zip(solo, guests, solo_lines):
         solved = solve_lines(lines, table, kernel, place == 0)
         arrived = exchange(after(solved, arrived))
         field = multiplicity(partners) * backward(arrived)
         total = total + weight(partners) * guest * field
-        total = total + moved(weight(groups) * owned * field, "band", partners)
+        partial = flattened(weight(groups) * owned * field)
+        partials.append(partial)
+        returned.append(moved(partial, "band", partners))
     if shared:
         solved = solve_lines(half_lines, table, half_kernel, (place == 0) & (half == 0))
         arrived = exchange(after(solved, arrived))
         half_back = arrived
-        other_back = moved(half_back, "band", opposite)
+        flat_back = flattened(half_back)
+        other_back = moved(flat_back, "band", opposite).reshape(half_back.shape)
+        partials.append(flat_back)
         own_part = along_y(along_z(from_blocks(half_back, half_rows), table), half_table.T)
         other_part = along_y(along_z(from_blocks(other_back, half_rows), table), other_table.T)
         scale = multiplicity(opposite) * weight(opposite)
         total = total + scale * far_guest * (own_part + other_part)
     solved = solve_lines(lines_self, table, kernel, place == 0)
-    field = backward(exchange(after(solved, arrived)))
+    field = backward(exchange(after(solved, arrived, *partials)))
+    for partial in returned:
+        total = total + partial.reshape(owned.shape)
     return -(total + weight(groups) * owned * field)[None]
 
 

time: 770 us -> 619 us (0.80)
  waiting for transfers between devices: 504 us -> 348 us
  other arithmetic: 28.7 us -> 37 us
    all_to_all x6, waiting for transfers between devices: 253 us -> 95.6 us  [exchange(): lax.all_to_all(blocks, 'space', split_axis=0, concat_axis=0, tiled=True)]
    reshape x7 -> x6, local copies, waits for them, and re-layouts: 25.6 us -> 23.8 us  [the longest x2 7.07 us: flattened(): return array.reshape(-1, 128)]
  transfers between devices with their start and end apart: 10 -> 10, of which waited for: 9 -> 6; matrix products, arithmetic and copies ran while one was open for 17% -> 25% of each run, Pallas kernels for 0% -> 0%
where the time goes in v3:
time: 619 us; the launch traced here: 610 us
  waiting for transfers between devices  348 us (56%)
  matrix products  94 us (15%)
  local copies, waits for them, and re-layouts  83.9 us (14%)
  other arithmetic  37 us (6%)
  starting transfers between devices  36.8 us (6%)
  between operations  9.84 us (2%)
    ppermute x4, waiting for transfers between devices, moved(): return lax.ppermute(flat, axis, list(enumerate(targets)))  253 us
    all_to_all x6, waiting for transfers between devices, exchange(): lax.all_to_all(blocks, 'space', split_axis=0, concat_axis=0, tiled=True)  95.6 us
    dot_general x7, matrix products, along_y(): return jnp.einsum('xyz,ky->xkz', field, table, precision=PRECISION)  36.9 us
    dot_general x7, matrix products, along_z(): return jnp.einsum('xyz,kz->xyk', field, table, precision=PRECISION)  30.7 us
    all_to_all x6, starting transfers between devices, exchange(): lax.all_to_all(blocks, 'space', split_axis=0, concat_axis=0, tiled=True)  29.3 us
    dot_general x6, matrix products, along_x(): return jnp.einsum('xn,kx->kn', lines, table, precision=PRECISION)  26.5 us
    reshape x6, local copies, waits for them, and re-layouts, to_blocks(): spectra.reshape(slab_rows, space_count, rows // space_count * length)  20.9 us
    reshape x4, local copies, waits for them, and re-layouts, from_blocks(): return blocks.transpose(1, 0, 2).reshape(slab_rows, rows, -1)  14.7 us
  transfers between devices with their start and end apart: 10, of which 6 were waited for; matrix products, arithmetic and copies ran while one was open for 25% of the time, Pallas kernels for 0%

profile of v3, /device:TPU:0, one launch (start us, length us, event | category | flops | bytes accessed | tf_op | source)
XLA Modules:
  0.0 610.0 jit_solution(4412965433810095582)
XLA Ops:
  5.5 5.3 fusion.13
  10.9 5.7 add_bitcast_fusion.1
  24.3 6.3 %all-to-all-start = ((f32[8,24,4608]{2,1,0:T(8,128)}), f32[8,24,4608]{2,1,0:T(8,128)}, u32[]{:S(2)}, u32[]{:S(2)}) async-start(f32[8,24,4608]{2,1,0:T(8,128)} %bitcast.125), calls=%async_computation | async-start | bytes 7077888 | tf_op jit(solution)/shard_map/all_to_all | solution.py:60
  37.1 77.5 %collective-permute-done = f32[6912,128]{1,0:T(8,128)} collective-permute-done((f32[6912,128]{1,0:T(8,128)S(1)}, f32[6912,128]{1,0:T(8,128)}, u32[]{:S(2)}, u32[]{:S(2)}) %collective-permute-start) | collective-permute-done | bytes 3538976 | tf_op jit(solution)/shard_map/ppermute | solution.py:13
  119.7 5.7 fusion.25
  126.7 6.7 %fusion.11 = f32[24,192,192]{2,1,0:T(8,128)S(1)} fusion(f32[]{:T(128)S(6)} %div.47, f32[24,192,192]{2,1,0:T(8,128)} %reshape.171, f32[1,24,192,192]{3,2,1,0:T(8,128)} %param.8), kind=kOutput, calls=%fused_computation.19 | convolution fusion | flops 1021353984 | bytes 10616836 | tf_op jit(solution)/shard_map/xyz,kz->xyk/dot_general | solution.py:48
  133.5 5.7 add_bitcast_fusion
  146.9 5.2 all-to-all-start.1
  156.1 76.0 %collective-permute-done.1 = f32[6912,128]{1,0:T(8,128)} collective-permute-done((f32[6912,128]{1,0:T(8,128)S(1)}, f32[6912,128]{1,0:T(8,128)}, u32[]{:S(2)}, u32[]{:S(2)}) %collective-permute-start.1) | collective-permute-done | bytes 3538976 | tf_op jit(solution)/shard_map/ppermute | solution.py:13
  237.2 5.6 fusion.26
  243.6 5.3 fusion.9
  266.8 5.5 convolution_multiply_fusion.1
  276.7 26.6 %all-to-all-done.2 = f32[8,24,2304]{2,1,0:T(8,128)S(1)} async-done(((f32[8,24,2304]{2,1,0:T(8,128)}), f32[8,24,2304]{2,1,0:T(8,128)S(1)}, u32[]{:S(2)}, u32[]{:S(2)}) %all-to-all-start.2) | async-done | bytes 1769504 | tf_op jit(solution)/shard_map/all_to_all | solution.py:60
  319.2 69.0 %all-to-all-done.3 = f32[8,24,4608]{2,1,0:T(8,128)S(1)} async-done(((f32[8,24,4608]{2,1,0:T(8,128)}), f32[8,24,4608]{2,1,0:T(8,128)S(1)}, u32[]{:S(2)}, u32[]{:S(2)}) %all-to-all-start.3) | async-done | bytes 3538976 | tf_op jit(solution)/shard_map/all_to_all | solution.py:60
  400.7 5.5 convolution_multiply_fusion
  414.7 5.6 reshape.177
  420.3 5.7 fusion.45
  426.0 7.7 %fusion.16 = (f32[24,192,192]{2,1,0:T(8,128)}, f32[24,192,192]{2,1,0:T(8,128)}) fusion(f32[1,24,192,192]{3,2,1,0:T(8,128)S(1)} %bitcast.128, f32[]{:T(128)} %bitcast.25, f32[]{:T(128)} %bitcast.6, f32[192,24,192]{2,0,1:T(8,128)S(1)} %fusion.45), kind=kOutput, calls=%fused_computation.25 | convolution fusion | flops 1022238720 | bytes 14155784 | tf_op jit(solution)/shard_map/xyz,kz->xyk/dot_general | solution.py:48
  433.8 5.7 reshape.184
  459.7 65.5 %collective-permute-done.3 = f32[6912,128]{1,0:T(8,128)} collective-permute-done((f32[6912,128]{1,0:T(8,128)}, f32[6912,128]{1,0:T(8,128)}, u32[]{:S(2)}, u32[]{:S(2)}) %collective-permute-start.3) | collective-permute-done | bytes 3538976 | tf_op jit(solution)/shard_map/ppermute | solution.py:13
  530.2 33.8 %collective-permute-done.2 = f32[3456,128]{1,0:T(8,128)} collective-permute-done((f32[3456,128]{1,0:T(8,128)}, f32[3456,128]{1,0:T(8,128)}, u32[]{:S(2)}, u32[]{:S(2)}) %collective-permute-start.2) | collective-permute-done | bytes 1769504 | tf_op jit(solution)/shard_map/ppermute | solution.py:13
  584.2 5.7 fusion.38
  589.9 5.1 fusion
  595.1 14.4 %fusion.6 = f32[1,24,192,192]{3,2,1,0:T(8,128)} fusion(f32[24,192,192]{2,1,0:T(8,128)} %reshape.185, f32[24,192,192]{2,1,0:T(8,128)} %fusion, f32[192,24,192]{2,0,1:T(8,128)} %fusion.57, f32[192,24,192]{2,0,1:T(8,128)} %fusion.55, f32[24,192,192]{2,1,0:T(8,128)S(1)} %bitcast.132, f32[24,192,192]{2,1,0:T(8,128)S(1)} %bitcast.134, ...), kind=kLoop, calls=%fused_computation.9 | loop fusion | flops 10616832 | bytes 31850512 | tf_op jit(solution)/shard_map/neg | solution.py:194
  (116 shorter events, 139.1 us)
Async XLA Ops:
  24.3 122.6 %all-to-all-start = ((f32[8,24,4608]{2,1,0:T(8,128)}), f32[8,24,4608]{2,1,0:T(8,128)}, u32[]{:S(2)}, u32[]{:S(2)}) async-start(f32[8,24,4608]{2,1,0:T(8,128)} %bitcast.125), calls=%async_computation | async-start | bytes 7077888 | tf_op jit(solution)/shard_map/all_to_all | solution.py:60
  35.1 84.6 %copy-start.2 = (f32[6912,128]{1,0:T(8,128)}, f32[6912,128]{1,0:T(8,128)S(1)}, u32[]{:S(2)}) copy-start(f32[6912,128]{1,0:T(8,128)S(1)} %reshape_squeeze.3) | copy-start | bytes 10616836
  35.1 79.6 %collective-permute-start = (f32[6912,128]{1,0:T(8,128)S(1)}, f32[6912,128]{1,0:T(8,128)}, u32[]{:S(2)}, u32[]{:S(2)}) collective-permute-start(f32[6912,128]{1,0:T(8,128)S(1)} %reshape_squeeze.3), channel_id=1, source_target_pairs={{0,16},{8,0},{16,24},{24,8},{1,17},{9,1},{17,25},{25,9},{2,18},{10... | collective-permute-start | bytes 10616840 | tf_op jit(solution)/shard_map/ppermute | solution.py:13
  146.9 109.5 %all-to-all-start.1 = ((f32[8,24,4608]{2,1,0:T(8,128)}), f32[8,24,4608]{2,1,0:T(8,128)}, u32[]{:S(2)}, u32[]{:S(2)}) async-start(f32[8,24,4608]{2,1,0:T(8,128)} %bitcast.124), calls=%async_computation.1 | async-start | bytes 7077888 | tf_op jit(solution)/shard_map/all_to_all | solution.py:60
  152.1 80.0 %collective-permute-start.1 = (f32[6912,128]{1,0:T(8,128)S(1)}, f32[6912,128]{1,0:T(8,128)}, u32[]{:S(2)}, u32[]{:S(2)}) collective-permute-start(f32[6912,128]{1,0:T(8,128)S(1)} %copy-done.3), channel_id=1, source_target_pairs={{0,24},{8,16},{16,8},{24,0},{1,25},{9,17},{17,9},{25,1},{2,26},{10... | collective-permute-start | bytes 10616840 | tf_op jit(solution)/shard_map/ppermute | solution.py:13
  237.2 6.4 %copy-start.5 = (f32[192,192]{1,0:T(8,128)S(1)}, f32[192,192]{1,0:T(8,128)}, u32[]{:S(2)}) copy-start(f32[192,192]{1,0:T(8,128)} %sine_add_fusion) | copy-start | bytes 442372
  256.4 47.0 %all-to-all-start.2 = ((f32[8,24,2304]{2,1,0:T(8,128)}), f32[8,24,2304]{2,1,0:T(8,128)S(1)}, u32[]{:S(2)}, u32[]{:S(2)}) async-start(f32[8,24,2304]{2,1,0:T(8,128)} %bitcast.126), calls=%async_computation.2 | async-start | bytes 3538944 | tf_op jit(solution)/shard_map/all_to_all | solution.py:60
  261.4 10.9 %copy-start.9 = (s32[192]{0:T(256)}, s32[192]{0:T(256)S(1)}, u32[]{:S(2)}) copy-start(s32[192]{0:T(256)S(1)} %fusion.71) | copy-start | bytes 2308
  261.5 10.8 %copy-start.7 = (s32[4608]{0:T(1024)}, s32[4608]{0:T(1024)S(1)}, u32[]{:S(2)}) copy-start(s32[4608]{0:T(1024)S(1)} %mul.243) | copy-start | bytes 55300
  261.6 10.7 %copy-start.8 = (s32[4608]{0:T(1024)}, s32[4608]{0:T(1024)S(1)}, u32[]{:S(2)}) copy-start(s32[4608]{0:T(1024)S(1)} %mul.242) | copy-start | bytes 55300
  304.6 83.6 %all-to-all-start.3 = ((f32[8,24,4608]{2,1,0:T(8,128)}), f32[8,24,4608]{2,1,0:T(8,128)S(1)}, u32[]{:S(2)}, u32[]{:S(2)}) async-start(f32[8,24,4608]{2,1,0:T(8,128)} %bitcast.138), calls=%async_computation.3 | async-start | bytes 7077888 | tf_op jit(solution)/shard_map/all_to_all | solution.py:60
  316.3 80.3 %copy-start.13 = (s32[4]{0:T(128)S(1)}, s32[4]{0:T(128)}, u32[]{:S(2)}) copy-start(s32[4]{0:T(128)} %constant.96.clone) | copy-start | bytes 52
  316.3 81.9 %copy-start.11 = (s32[4]{0:T(128)S(1)}, s32[4]{0:T(128)}, u32[]{:S(2)}) copy-start(s32[4]{0:T(128)} %param.9) | copy-start | bytes 52
  316.3 81.9 %copy-start.12 = (f32[4]{0:T(128)S(1)}, f32[4]{0:T(128)}, u32[]{:S(2)}) copy-start(f32[4]{0:T(128)} %constant.93.clone) | copy-start | bytes 52
  316.3 84.4 %copy-start.10 = (s32[192]{0:T(256)S(1)}, s32[192]{0:T(256)}, u32[]{:S(2)}) copy-start(s32[192]{0:T(256)} %copy-done.9) | copy-start | bytes 2308
  390.0 49.5 %all-to-all-start.4 = ((f32[8,24,2304]{2,1,0:T(8,128)}), f32[8,24,2304]{2,1,0:T(8,128)S(1)}, u32[]{:S(2)}, u32[]{:S(2)}) async-start(f32[8,24,2304]{2,1,0:T(8,128)} %bitcast.139), calls=%async_computation.4 | async-start | bytes 3538944 | tf_op jit(solution)/shard_map/all_to_all | solution.py:60
  414.7 11.3 %slice-start = ((s8[4718592]{0:T(1024)(128)(4,1)}), s8[524288]{0:T(1024)(128)(4,1)S(1)}, s32[]{:S(2)}) async-start(s8[4718592]{0:T(1024)(128)(4,1)} %bitcast.127), calls=%async_computation.6 | async-start | bytes 1048576
  420.3 5.7 slice-start.1
  440.8 135.6 %all-to-all-start.5 = ((f32[8,24,4608]{2,1,0:T(8,128)}), f32[8,24,4608]{2,1,0:T(8,128)}, u32[]{:S(2)}, u32[]{:S(2)}) async-start(f32[8,24,4608]{2,1,0:T(8,128)} %bitcast.137), calls=%async_computation.5 | async-start | bytes 7077888 | tf_op jit(solution)/shard_map/all_to_all | solution.py:60
  445.9 79.3 %collective-permute-start.3 = (f32[6912,128]{1,0:T(8,128)}, f32[6912,128]{1,0:T(8,128)}, u32[]{:S(2)}, u32[]{:S(2)}) collective-permute-start(f32[6912,128]{1,0:T(8,128)} %reshape.184), channel_id=1, source_target_pairs={{0,8},{8,24},{16,0},{24,16},{1,9},{9,25},{17,1},{25,17},{2,10},{10... | collective-permute-start | bytes 10616840 | tf_op jit(solution)/shard_map/ppermute | solution.py:13
  447.4 116.6 %collective-permute-start.2 = (f32[3456,128]{1,0:T(8,128)}, f32[3456,128]{1,0:T(8,128)}, u32[]{:S(2)}, u32[]{:S(2)}) collective-permute-start(f32[3456,128]{1,0:T(8,128)} %reshape.181), channel_id=1, source_target_pairs={{0,24},{8,16},{16,8},{24,0},{1,25},{9,17},{17,9},{25,1},{2,26},{10... | collective-permute-start | bytes 5308424 | tf_op jit(solution)/shard_map/ppermute | solution.py:13
  584.1 10.9 %slice-start.2 = ((s8[4718592]{0:T(1024)(128)(4,1)}), s8[4194304]{0:T(1024)(128)(4,1)S(1)}, s32[]{:S(2)}) async-start(s8[4718592]{0:T(1024)(128)(4,1)} %bitcast.129), calls=%async_computation.8 | async-start | bytes 8388608
  584.1 10.9 %slice-start.4 = ((s8[4718592]{0:T(1024)(128)(4,1)}), s8[4194304]{0:T(1024)(128)(4,1)S(1)}, s32[]{:S(2)}) async-start(s8[4718592]{0:T(1024)(128)(4,1)} %bitcast.131), calls=%async_computation.10 | async-start | bytes 8388608
  584.2 10.9 %slice-start.6 = ((s8[4718592]{0:T(1024)(128)(4,1)}), s8[4194304]{0:T(1024)(128)(4,1)S(1)}, s32[]{:S(2)}) async-start(s8[4718592]{0:T(1024)(128)(4,1)} %bitcast.133), calls=%async_computation.12 | async-start | bytes 8388608
  (8 other events, 32.9 us)

commit v4 on v3

--- a/solution.py
+++ b/solution.py
@@ -134,19 +134,26 @@
         return [groups.index(g) for g in range(group_count)]
 
     groups = list(range(group_count))
-    flat_guests = []
-    source = flattened(owned)
-    for partners in solo + ([opposite] if shared else []):
-        flat_guests.append(moved(source, "band", inverse(partners)))
-        source = after(source, flat_guests[-1])
-
-    blocks = forward(owned * owned)
+    early_planes = max(1, owned.shape[0] // 4)
+    back = inverse(solo[0])
+    early = moved(flattened(owned[:early_planes]), "band", back)
+    late = moved(after(flattened(owned[early_planes:]), early), "band", back)
+    flat_guests = [(early, late)]
+    for partners in solo[1:] + ([opposite] if shared else []):
+        source = after(flattened(owned), *flat_guests[-1])
+        flat_guests.append((moved(source, "band", inverse(partners)),))
+
+    def assembled(parts, *earlier):
+        parts = lax.optimization_barrier(parts + earlier)[: len(parts)]
+        return jnp.concatenate([part.reshape((-1,) + owned.shape[1:]) for part in parts])
+
+    blocks = after(forward(owned * owned), early)
     arrived = exchange(blocks)
     lines_self = arrived
     guests = []
     solo_lines = []
     for index in range(len(solo)):
-        guests.append(after(flat_guests[index], blocks).reshape(owned.shape))
+        guests.append(assembled(flat_guests[index], blocks))
         blocks = after(forward(owned * guests[index]), arrived)
         arrived = exchange(blocks)
         solo_lines.append(arrived)
@@ -157,7 +164,7 @@
         half_table = lax.dynamic_slice_in_dim(table, half * half_rows, half_rows, 0)
         other_table = lax.dynamic_slice_in_dim(table, (1 - half) * half_rows, half_rows, 0)
         half_kernel = kernel_block(length, half * half_rows + place * half_count, half_count)
-        far_guest = after(flat_guests[-1], blocks).reshape(owned.shape)
+        far_guest = assembled(flat_guests[-1], blocks)
         density = owned * far_guest
         level = jnp.mean(density)
         spectra = along_z(along_y(density - level, half_table), table)
@@ -166,32 +173,26 @@
         half_lines = arrived
 
     total = jnp.zeros_like(owned)
-    partials = []
-    returned = []
+    if shared:
+        solved = solve_lines(half_lines, table, half_kernel, (place == 0) & (half == 0))
+        half_back = exchange(after(solved, arrived))
+        arrived = half_back
+        other_back = moved(flattened(half_back), "band", opposite).reshape(half_back.shape)
     for partners, guest, lines in zip(solo, guests, solo_lines):
         solved = solve_lines(lines, table, kernel, place == 0)
         arrived = exchange(after(solved, arrived))
         field = multiplicity(partners) * backward(arrived)
         total = total + weight(partners) * guest * field
         partial = flattened(weight(groups) * owned * field)
-        partials.append(partial)
-        returned.append(moved(partial, "band", partners))
-    if shared:
-        solved = solve_lines(half_lines, table, half_kernel, (place == 0) & (half == 0))
-        arrived = exchange(after(solved, arrived))
-        half_back = arrived
-        flat_back = flattened(half_back)
-        other_back = moved(flat_back, "band", opposite).reshape(half_back.shape)
-        partials.append(flat_back)
+        total = total + moved(partial, "band", partners).reshape(owned.shape)
+    if shared:
         own_part = along_y(along_z(from_blocks(half_back, half_rows), table), half_table.T)
         other_part = along_y(along_z(from_blocks(other_back, half_rows), table), other_table.T)
         scale = multiplicity(opposite) * weight(opposite)
         total = total + scale * far_guest * (own_part + other_part)
     solved = solve_lines(lines_self, table, kernel, place == 0)
-    field = backward(exchange(after(solved, arrived, *partials)))
-    for partial in returned:
-        total = total + partial.reshape(owned.shape)
-    return -(total + weight(groups) * owned * field)[None]
+    field = backward(exchange(after(solved, arrived)))
+    return -(after(total) + weight(groups) * owned * field)[None]
 
 
 def solution(mesh):

time: 619 us -> 653 us (1.055)
  waiting for transfers between devices: 348 us -> 378 us
  local copies, waits for them, and re-layouts: 83.9 us -> 92.4 us
    all_to_all x6, waiting for transfers between devices: 95.6 us -> 139 us  [exchange(): lax.all_to_all(blocks, 'space', split_axis=0, concat_axis=0, tiled=True)]
    add x0 -> x1, other arithmetic: none -> 14.4 us  [shards(): total = total + scale * far_guest * (own_part + other_part)]
    ppermute x4 -> x5, waiting for transfers between devices: 253 us -> 239 us  [moved(): return lax.ppermute(flat, axis, list(enumerate(targets)))]
    neg x1, other arithmetic: 14.4 us -> 3.92 us  [shards(): return -(after(total) + weight(groups) * owned * field)[None]]
    reshape x4 -> x5, local copies, waits for them, and re-layouts: 16.7 us -> 15.8 us  [the longest x3 8.97 us: assembled(): part.reshape((-1,) + owned.shape[1:])]
  transfers between devices with their start and end apart: 10 -> 11, of which waited for: 6 -> 6; matrix products, arithmetic and copies ran while one was open for 25% -> 29% of each run, Pallas kernels for 0% -> 0%
where the time goes in v4:
time: 653 us; the launch traced here: 643 us
  waiting for transfers between devices  378 us (58%)
  local copies, waits for them, and re-layouts  92.4 us (14%)
  matrix products  90.2 us (14%)
  starting transfers between devices  37.4 us (6%)
  other arithmetic  35.7 us (5%)
  between operations  9.97 us (2%)
    ppermute x5, waiting for transfers between devices, moved(): return lax.ppermute(flat, axis, list(enumerate(targets)))  239 us
    all_to_all x6, waiting for transfers between devices, exchange(): lax.all_to_all(blocks, 'space', split_axis=0, concat_axis=0, tiled=True)  139 us
    dot_general x7, matrix products, along_y(): return jnp.einsum('xyz,ky->xkz', field, table, precision=PRECISION)  36.8 us
    dot_general x7, matrix products, along_z(): return jnp.einsum('xyz,kz->xyk', field, table, precision=PRECISION)  28.4 us
    all_to_all x6, starting transfers between devices, exchange(): lax.all_to_all(blocks, 'space', split_axis=0, concat_axis=0, tiled=True)  28.1 us
    dot_general x6, matrix products, along_x(): return jnp.einsum('xn,kx->kn', lines, table, precision=PRECISION)  25 us
    reshape x6, local copies, waits for them, and re-layouts, to_blocks(): spectra.reshape(slab_rows, space_count, rows // space_count * length)  20.8 us
    add x1, other arithmetic, shards(): total = total + scale * far_guest * (own_part + other_part)  14.4 us
  transfers between devices with their start and end apart: 11, of which 6 were waited for; matrix products, arithmetic and copies ran while one was open for 29% of the time, Pallas kernels for 0%

profile of v4, /device:TPU:0, one launch (start us, length us, event | category | flops | bytes accessed | tf_op | source)
XLA Modules:
  0.0 643.4 jit_solution(4578519764410123194)
XLA Ops:
  11.4 5.3 fusion.9
  16.7 5.7 add_bitcast_fusion.1
  41.9 58.8 %collective-permute-done.1 = f32[5184,128]{1,0:T(8,128)} collective-permute-done((f32[5184,128]{1,0:T(8,128)}, f32[5184,128]{1,0:T(8,128)}, u32[]{:S(2)}, u32[]{:S(2)}) %collective-permute-start.1) | collective-permute-done | bytes 2654240 | tf_op jit(solution)/shard_map/ppermute | solution.py:13
  114.8 6.7 %fusion.7 = f32[24,192,192]{2,1,0:T(8,128)S(1)} fusion(f32[]{:T(128)S(6)} %div.47, f32[24,192,192]{2,1,0:T(8,128)} %copy-done, f32[1,24,192,192]{3,2,1,0:T(8,128)} %param.8), kind=kOutput, calls=%fused_computation.16 | convolution fusion | flops 1021353984 | bytes 10616836 | tf_op jit(solution)/shard_map/xyz,kz->xyk/dot_general | solution.py:48
  121.5 5.7 add_bitcast_fusion
  139.9 5.7 reshape_squeeze.3
  148.5 77.1 %collective-permute-done.2 = f32[6912,128]{1,0:T(8,128)S(1)} collective-permute-done((f32[6912,128]{1,0:T(8,128)}, f32[6912,128]{1,0:T(8,128)S(1)}, u32[]{:S(2)}, u32[]{:S(2)}) %collective-permute-start.2) | collective-permute-done | bytes 3538976 | tf_op jit(solution)/shard_map/ppermute | solution.py:13
  228.7 5.6 fusion.22
  235.0 5.3 fusion.5
  247.8 5.0 all-to-all-start.2
  253.0 41.7 %all-to-all-done.2 = f32[8,24,2304]{2,1,0:T(8,128)S(1)} async-done(((f32[8,24,2304]{2,1,0:T(8,128)}), f32[8,24,2304]{2,1,0:T(8,128)S(1)}, u32[]{:S(2)}, u32[]{:S(2)}) %all-to-all-start.2) | async-done | bytes 1769504 | tf_op jit(solution)/shard_map/all_to_all | solution.py:60
  309.6 5.5 convolution_multiply_fusion.1
  319.6 27.1 %all-to-all-done.3 = f32[8,24,2304]{2,1,0:T(8,128)S(1)} async-done(((f32[8,24,2304]{2,1,0:T(8,128)}), f32[8,24,2304]{2,1,0:T(8,128)S(1)}, u32[]{:S(2)}, u32[]{:S(2)}) %all-to-all-start.3) | async-done | bytes 1769504 | tf_op jit(solution)/shard_map/all_to_all | solution.py:60
  351.7 5.5 convolution_multiply_fusion
  361.7 69.9 %all-to-all-done.4 = f32[8,24,4608]{2,1,0:T(8,128)} async-done(((f32[8,24,4608]{2,1,0:T(8,128)}), f32[8,24,4608]{2,1,0:T(8,128)}, u32[]{:S(2)}, u32[]{:S(2)}) %all-to-all-start.4) | async-done | bytes 3538976 | tf_op jit(solution)/shard_map/all_to_all | solution.py:60
  442.6 5.8 copy.37
  448.5 5.5 reshape.195
  454.0 5.7 fusion.41
  459.7 7.6 %fusion.12 = (f32[24,192,192]{2,1,0:T(8,128)}, f32[24,192,192]{2,1,0:T(8,128)}) fusion(f32[1,24,192,192]{3,2,1,0:T(8,128)S(1)} %bitcast.126, f32[]{:T(128)} %bitcast.18, f32[]{:T(128)} %bitcast.6, f32[192,24,192]{2,0,1:T(8,128)S(1)} %fusion.41), kind=kOutput, calls=%fused_computation.22 | convolution fusion | flops 1022238720 | bytes 14155784 | tf_op jit(solution)/shard_map/xyz,kz->xyk/dot_general | solution.py:48
  467.3 5.7 reshape.196
  488.1 103.0 %collective-permute-done.4 = f32[3456,128]{1,0:T(8,128)} collective-permute-done((f32[3456,128]{1,0:T(8,128)}, f32[3456,128]{1,0:T(8,128)}, u32[]{:S(2)}, u32[]{:S(2)}) %collective-permute-start.4) | collective-permute-done | bytes 1769504 | tf_op jit(solution)/shard_map/ppermute | solution.py:13
  603.2 5.3 reshape.197
  608.5 14.4 %fusion.2 = f32[24,192,192]{2,1,0:T(8,128)} fusion(f32[192,24,192]{2,0,1:T(8,128)} %fusion.53, f32[192,24,192]{2,0,1:T(8,128)} %fusion.51, f32[24,192,192]{2,1,0:T(8,128)} %reshape.191, f32[24,192,192]{2,1,0:T(8,128)} %reshape.197, f32[24,192,192]{2,1,0:T(8,128)} %copy-done, f32[24,192,192]{2,1,0:T(8,128)} %get-tuple-element.31, f32[]{:T(128)} %bitcast.20, ...), kind=kLoop, calls=%fused_computation.5 | loop fusion | flops 7077888 | bytes 24772620 | tf_op jit(solution)/shard_map/add | solution.py:192
  630.3 5.7 fusion.34
  (111 shorter events, 143.9 us)
Async XLA Ops:
  2.9 27.3 %collective-permute-start = (f32[1728,128]{1,0:T(8,128)}, f32[1728,128]{1,0:T(8,128)}, u32[]{:S(2)}, u32[]{:S(2)}) collective-permute-start(f32[1728,128]{1,0:T(8,128)} %reshape.183), channel_id=1, source_target_pairs={{0,16},{8,0},{16,24},{24,8},{1,17},{9,1},{17,25},{25,9},{2,18},{10... | collective-permute-start | bytes 2654216 | tf_op jit(solution)/shard_map/ppermute | solution.py:13
  30.1 104.8 %all-to-all-start = ((f32[8,24,4608]{2,1,0:T(8,128)}), f32[8,24,4608]{2,1,0:T(8,128)}, u32[]{:S(2)}, u32[]{:S(2)}) async-start(f32[8,24,4608]{2,1,0:T(8,128)} %bitcast.121), calls=%async_computation | async-start | bytes 7077888 | tf_op jit(solution)/shard_map/all_to_all | solution.py:60
  39.9 60.7 %collective-permute-start.1 = (f32[5184,128]{1,0:T(8,128)}, f32[5184,128]{1,0:T(8,128)}, u32[]{:S(2)}, u32[]{:S(2)}) collective-permute-start(f32[5184,128]{1,0:T(8,128)} %reshape.184), channel_id=1, source_target_pairs={{0,16},{8,0},{16,24},{24,8},{1,17},{9,1},{17,25},{25,9},{2,18},{10... | collective-permute-start | bytes 7962632 | tf_op jit(solution)/shard_map/ppermute | solution.py:13
  102.1 9.4 %slice-start = ((s8[4718592]{0:T(1024)(128)(4,1)}), s8[524288]{0:T(1024)(128)(4,1)S(1)}, s32[]{:S(2)}) async-start(s8[4718592]{0:T(1024)(128)(4,1)} %bitcast.123), calls=%async_computation.6 | async-start | bytes 1048576
  106.7 4.8 slice-start.1
  134.9 112.8 %all-to-all-start.1 = ((f32[8,24,4608]{2,1,0:T(8,128)}), f32[8,24,4608]{2,1,0:T(8,128)}, u32[]{:S(2)}, u32[]{:S(2)}) async-start(f32[8,24,4608]{2,1,0:T(8,128)} %bitcast.120), calls=%async_computation.1 | async-start | bytes 7077888 | tf_op jit(solution)/shard_map/all_to_all | solution.py:60
  145.6 80.0 %collective-permute-start.2 = (f32[6912,128]{1,0:T(8,128)}, f32[6912,128]{1,0:T(8,128)S(1)}, u32[]{:S(2)}, u32[]{:S(2)}) collective-permute-start(f32[6912,128]{1,0:T(8,128)} %reshape_squeeze.3), channel_id=1, source_target_pairs={{0,24},{8,16},{16,8},{24,0},{1,25},{9,17},{17,9},{25,1},{2,26},{10... | collective-permute-start | bytes 10616840 | tf_op jit(solution)/shard_map/ppermute | solution.py:13
  228.7 6.4 copy-start.1
  247.8 47.0 %all-to-all-start.2 = ((f32[8,24,2304]{2,1,0:T(8,128)}), f32[8,24,2304]{2,1,0:T(8,128)S(1)}, u32[]{:S(2)}, u32[]{:S(2)}) async-start(f32[8,24,2304]{2,1,0:T(8,128)} %bitcast.122), calls=%async_computation.2 | async-start | bytes 3538944 | tf_op jit(solution)/shard_map/all_to_all | solution.py:60
  301.2 45.6 %all-to-all-start.3 = ((f32[8,24,2304]{2,1,0:T(8,128)}), f32[8,24,2304]{2,1,0:T(8,128)S(1)}, u32[]{:S(2)}, u32[]{:S(2)}) async-start(f32[8,24,2304]{2,1,0:T(8,128)} %bitcast.134), calls=%async_computation.3 | async-start | bytes 3538944 | tf_op jit(solution)/shard_map/all_to_all | solution.py:60
  346.7 84.9 %all-to-all-start.4 = ((f32[8,24,4608]{2,1,0:T(8,128)}), f32[8,24,4608]{2,1,0:T(8,128)}, u32[]{:S(2)}, u32[]{:S(2)}) async-start(f32[8,24,4608]{2,1,0:T(8,128)} %bitcast.133), calls=%async_computation.4 | async-start | bytes 7077888 | tf_op jit(solution)/shard_map/all_to_all | solution.py:60
  431.6 4.8 copy-start.5
  431.6 6.7 %copy-start.4 = (s32[4]{0:T(128)S(1)}, s32[4]{0:T(128)}, u32[]{:S(2)}) copy-start(s32[4]{0:T(128)} %constant.96.clone) | copy-start | bytes 52
  431.6 8.6 %copy-start.2 = (s32[4]{0:T(128)S(1)}, s32[4]{0:T(128)}, u32[]{:S(2)}) copy-start(s32[4]{0:T(128)} %param.9) | copy-start | bytes 52
  431.6 8.6 %copy-start.3 = (f32[4]{0:T(128)S(1)}, f32[4]{0:T(128)}, u32[]{:S(2)}) copy-start(f32[4]{0:T(128)} %constant.93.clone) | copy-start | bytes 52
  431.6 191.3 %all-to-all-start.5 = ((f32[8,24,4608]{2,1,0:T(8,128)}), f32[8,24,4608]{2,1,0:T(8,128)}, u32[]{:S(2)}, u32[]{:S(2)}) async-start(f32[8,24,4608]{2,1,0:T(8,128)} %bitcast.132), calls=%async_computation.5 | async-start | bytes 7077888 | tf_op jit(solution)/shard_map/all_to_all | solution.py:60
  448.5 11.2 %slice-start.2 = ((s8[4718592]{0:T(1024)(128)(4,1)}), s8[524288]{0:T(1024)(128)(4,1)S(1)}, s32[]{:S(2)}) async-start(s8[4718592]{0:T(1024)(128)(4,1)} %bitcast.125), calls=%async_computation.8 | async-start | bytes 1048576
  454.0 5.7 slice-start.3
  473.1 130.1 %collective-permute-start.3 = (f32[6912,128]{1,0:T(8,128)}, f32[6912,128]{1,0:T(8,128)}, u32[]{:S(2)}, u32[]{:S(2)}) collective-permute-start(f32[6912,128]{1,0:T(8,128)} %reshape.196), channel_id=1, source_target_pairs={{0,8},{8,24},{16,0},{24,16},{1,9},{9,25},{17,1},{25,17},{2,10},{10... | collective-permute-start | bytes 10616840 | tf_op jit(solution)/shard_map/ppermute | solution.py:13
  474.9 116.2 %collective-permute-start.4 = (f32[3456,128]{1,0:T(8,128)}, f32[3456,128]{1,0:T(8,128)}, u32[]{:S(2)}, u32[]{:S(2)}) collective-permute-start(f32[3456,128]{1,0:T(8,128)} %reshape.199), channel_id=1, source_target_pairs={{0,24},{8,16},{16,8},{24,0},{1,25},{9,17},{17,9},{25,1},{2,26},{10... | collective-permute-start | bytes 5308424 | tf_op jit(solution)/shard_map/ppermute | solution.py:13
  630.3 8.7 %slice-start.4 = ((s8[4718592]{0:T(1024)(128)(4,1)}), s8[4194304]{0:T(1024)(128)(4,1)S(1)}, s32[]{:S(2)}) async-start(s8[4718592]{0:T(1024)(128)(4,1)} %bitcast.127), calls=%async_computation.10 | async-start | bytes 8388608
  630.3 8.7 %slice-start.7 = ((s8[4718592]{0:T(1024)(128)(4,1)}), s8[4194304]{0:T(1024)(128)(4,1)S(1)}, s32[]{:S(2)}) async-start(s8[4718592]{0:T(1024)(128)(4,1)} %bitcast.129), calls=%async_computation.13 | async-start | bytes 8388608
  636.0 3.0 slice-start.5
  636.0 3.0 slice-start.8
  (2 other events, 4.1 us)

commit v5 on v4

--- a/solution.py
+++ b/solution.py
@@ -135,26 +135,29 @@
 
     groups = list(range(group_count))
     early_planes = max(1, owned.shape[0] // 4)
-    back = inverse(solo[0])
-    early = moved(flattened(owned[:early_planes]), "band", back)
-    late = moved(after(flattened(owned[early_planes:]), early), "band", back)
-    flat_guests = [(early, late)]
-    for partners in solo[1:] + ([opposite] if shared else []):
-        source = after(flattened(owned), *flat_guests[-1])
-        flat_guests.append((moved(source, "band", inverse(partners)),))
+    early_part = flattened(owned[:early_planes])
+    late_part = flattened(owned[early_planes:])
+    flat_guests = []
+    last = ()
+    for partners in solo + ([opposite] if shared else []):
+        early = moved(after(early_part, *last), "band", inverse(partners))
+        late = moved(after(late_part, early), "band", inverse(partners))
+        flat_guests.append((early, late))
+        last = (late,)
 
     def assembled(parts, *earlier):
         parts = lax.optimization_barrier(parts + earlier)[: len(parts)]
         return jnp.concatenate([part.reshape((-1,) + owned.shape[1:]) for part in parts])
 
-    blocks = after(forward(owned * owned), early)
+    blocks = after(forward(owned * owned), flat_guests[0][0])
     arrived = exchange(blocks)
     lines_self = arrived
     guests = []
     solo_lines = []
     for index in range(len(solo)):
         guests.append(assembled(flat_guests[index], blocks))
-        blocks = after(forward(owned * guests[index]), arrived)
+        early = [parts[0] for parts in flat_guests[index + 1 : index + 2]]
+        blocks = after(forward(owned * guests[index]), arrived, *early)
         arrived = exchange(blocks)
         solo_lines.append(arrived)
     if shared:
@@ -173,18 +176,21 @@
         half_lines = arrived
 
     total = jnp.zeros_like(owned)
+    away = []
+    returned = []
     if shared:
         solved = solve_lines(half_lines, table, half_kernel, (place == 0) & (half == 0))
         half_back = exchange(after(solved, arrived))
         arrived = half_back
-        other_back = moved(flattened(half_back), "band", opposite).reshape(half_back.shape)
+        away.append(moved(flattened(half_back), "band", opposite))
+        other_back = away[0].reshape(half_back.shape)
     for partners, guest, lines in zip(solo, guests, solo_lines):
         solved = solve_lines(lines, table, kernel, place == 0)
         arrived = exchange(after(solved, arrived))
-        field = multiplicity(partners) * backward(arrived)
+        field = multiplicity(partners) * backward(after(arrived, *away))
         total = total + weight(partners) * guest * field
         partial = flattened(weight(groups) * owned * field)
-        total = total + moved(partial, "band", partners).reshape(owned.shape)
+        returned.append(moved(partial, "band", partners))
     if shared:
         own_part = along_y(along_z(from_blocks(half_back, half_rows), table), half_table.T)
         other_part = along_y(along_z(from_blocks(other_back, half_rows), table), other_table.T)
@@ -192,7 +198,10 @@
         total = total + scale * far_guest * (own_part + other_part)
     solved = solve_lines(lines_self, table, kernel, place == 0)
     field = backward(exchange(after(solved, arrived)))
-    return -(after(total) + weight(groups) * owned * field)[None]
+    total = after(total) + weight(groups) * owned * field
+    for partial in returned:
+        total = total + partial.reshape(owned.shape)
+    return -total[None]
 
 
 def solution(mesh):

time: 653 us -> 576 us (0.88)
  waiting for transfers between devices: 378 us -> 297 us
  matrix products: 90.2 us -> 106 us
  other arithmetic: 35.7 us -> 21.1 us
    ppermute x5 -> x6, waiting for transfers between devices: 239 us -> 164 us  [moved(): return lax.ppermute(flat, axis, list(enumerate(targets)))]
    add x1 -> x0, other arithmetic: 14.4 us -> none  [shards(): total = total + scale * far_guest * (own_part + other_part)]
    dot_general x7, matrix products: 36.8 us -> 46.4 us  [along_y(): return jnp.einsum('xyz,ky->xkz', field, table, precision=PRECISION)]
  transfers between devices with their start and end apart: 11 -> 12, of which waited for: 6 -> 7; matrix products, arithmetic and copies ran while one was open for 29% -> 32% of each run, Pallas kernels for 0% -> 0%
where the time goes in v5:
time: 576 us; the launch traced here: 567 us
  waiting for transfers between devices  297 us (52%)
  matrix products  106 us (18%)
  local copies, waits for them, and re-layouts  94.9 us (16%)
  starting transfers between devices  38.8 us (7%)
  other arithmetic  21.1 us (4%)
  between operations  9.88 us (2%)
    ppermute x6, waiting for transfers between devices, moved(): return lax.ppermute(flat, axis, list(enumerate(targets)))  164 us
    all_to_all x6, waiting for transfers between devices, exchange(): lax.all_to_all(blocks, 'space', split_axis=0, concat_axis=0, tiled=True)  133 us
    dot_general x7, matrix products, along_y(): return jnp.einsum('xyz,ky->xkz', field, table, precision=PRECISION)  46.4 us
    dot_general x7, matrix products, along_z(): return jnp.einsum('xyz,kz->xyk', field, table, precision=PRECISION)  30.7 us
    dot_general x6, matrix products, along_x(): return jnp.einsum('xn,kx->kn', lines, table, precision=PRECISION)  28.5 us
    all_to_all x6, starting transfers between devices, exchange(): lax.all_to_all(blocks, 'space', split_axis=0, concat_axis=0, tiled=True)  28.2 us
    reshape x6, local copies, waits for them, and re-layouts, to_blocks(): spectra.reshape(slab_rows, space_count, rows // space_count * length)  20.9 us
    reshape x4, local copies, waits for them, and re-layouts, from_blocks(): return blocks.transpose(1, 0, 2).reshape(slab_rows, rows, -1)  14.3 us
  transfers between devices with their start and end apart: 12, of which 7 were waited for; matrix products, arithmetic and copies ran while one was open for 32% of the time, Pallas kernels for 0%

profile of v5, /device:TPU:0, one launch (start us, length us, event | category | flops | bytes accessed | tf_op | source)
XLA Modules:
  0.0 566.9 jit_solution(2301386492029432445)
XLA Ops:
  11.4 5.3 fusion.9
  16.7 5.7 %add_bitcast_fusion.1 = f32[24,192,192]{2,1,0:T(8,128)} fusion(f32[192,192]{1,0:T(8,128)S(1)} %and_select_fusion.1, f32[24,192,192]{2,1,0:T(8,128)S(1)} %fusion.9), kind=kOutput, calls=%fused_computation.18 | convolution fusion | flops 1020469248 | bytes 7225344 | tf_op jit(solution)/shard_map/xyz,ky->xkz/dot_general | solution.py:52
  41.9 58.8 %collective-permute-done.1 = f32[5184,128]{1,0:T(8,128)} collective-permute-done((f32[5184,128]{1,0:T(8,128)}, f32[5184,128]{1,0:T(8,128)}, u32[]{:S(2)}, u32[]{:S(2)}) %collective-permute-start.1) | collective-permute-done | bytes 2654240 | tf_op jit(solution)/shard_map/ppermute | solution.py:13
  116.4 6.7 %fusion.7 = f32[24,192,192]{2,1,0:T(8,128)S(1)} fusion(f32[]{:T(128)S(6)} %div.47, f32[24,192,192]{2,1,0:T(8,128)} %copy-done.1, f32[1,24,192,192]{3,2,1,0:T(8,128)} %param.8), kind=kOutput, calls=%fused_computation.16 | convolution fusion | flops 1021353984 | bytes 10616836 | tf_op jit(solution)/shard_map/xyz,kz->xyk/dot_general | solution.py:48
  123.2 5.7 %add_bitcast_fusion = f32[24,192,192]{2,1,0:T(8,128)} fusion(f32[192,192]{1,0:T(8,128)S(1)} %and_select_fusion, f32[24,192,192]{2,1,0:T(8,128)S(1)} %fusion.7), kind=kOutput, calls=%fused_computation.15 | convolution fusion | flops 1020469248 | bytes 7225344 | tf_op jit(solution)/shard_map/xyz,ky->xkz/dot_general | solution.py:52
  144.7 58.7 %collective-permute-done.3 = f32[5184,128]{1,0:T(8,128)} collective-permute-done((f32[5184,128]{1,0:T(8,128)S(1)}, f32[5184,128]{1,0:T(8,128)}, u32[]{:S(2)}, u32[]{:S(2)}) %collective-permute-start.3) | collective-permute-done | bytes 2654240 | tf_op jit(solution)/shard_map/ppermute | solution.py:13
  216.8 5.3 fusion.5
  234.9 41.7 %all-to-all-done.2 = f32[8,24,2304]{2,1,0:T(8,128)S(1)} async-done(((f32[8,24,2304]{2,1,0:T(8,128)}), f32[8,24,2304]{2,1,0:T(8,128)S(1)}, u32[]{:S(2)}, u32[]{:S(2)}) %all-to-all-start.2) | async-done | bytes 1769504 | tf_op jit(solution)/shard_map/all_to_all | solution.py:60
  291.4 5.5 convolution_multiply_fusion.1
  301.3 27.4 %all-to-all-done.3 = f32[8,24,2304]{2,1,0:T(8,128)S(1)} async-done(((f32[8,24,2304]{2,1,0:T(8,128)}), f32[8,24,2304]{2,1,0:T(8,128)S(1)}, u32[]{:S(2)}, u32[]{:S(2)}) %all-to-all-start.3) | async-done | bytes 1769504 | tf_op jit(solution)/shard_map/all_to_all | solution.py:60
  333.6 7.2 %convolution_multiply_fusion = f32[192,4608]{1,0:T(8,128)} fusion(f32[192,4608]{1,0:T(8,128)} %bitcast.26, f32[4608]{0:T(1024)S(1)} %get-tuple-element.38, s32[4608]{0:T(1024)S(1)} %mul.243, s32[4608]{0:T(1024)S(1)} %mul.242, s32[192]{0:T(256)S(1)} %fusion.66), kind=kOutput, calls=%fused_computation | convolution fusion | flops 1029316608 | bytes 7133952 | tf_op jit(solution)/shard_map/xn,kx->kn/dot_general | solution.py:56
  343.7 6.2 %fusion.57 = f32[192,4608]{1,0:T(8,128)} fusion(f32[192,4608]{1,0:T(8,128)} %convolution_multiply_fusion), kind=kOutput, calls=%fused_computation.80 | convolution fusion | flops 1019584512 | bytes 7077888 | tf_op jit(solution)/shard_map/xn,kx->kn/dot_general | solution.py:56
  349.9 63.7 %all-to-all-done.4 = f32[8,24,4608]{2,1,0:T(8,128)} async-done(((f32[8,24,4608]{2,1,0:T(8,128)}), f32[8,24,4608]{2,1,0:T(8,128)}, u32[]{:S(2)}, u32[]{:S(2)}) %all-to-all-start.4) | async-done | bytes 3538976 | tf_op jit(solution)/shard_map/all_to_all | solution.py:60
  424.7 5.8 %copy.38 = f32[24,8,4608]{2,1,0:T(8,128)} copy(f32[24,8,4608]{2,0,1:T(8,128)} %bitcast.16) | data formatting | bytes 7077888 | tf_op jit(solution)/shard_map/transpose | solution.py:72
  430.5 5.5 reshape.200
  436.0 5.7 %fusion.41 = f32[192,24,192]{2,0,1:T(8,128)S(1)} fusion(f32[24,192,192]{2,1,0:T(8,128)} %reshape.200), kind=kOutput, calls=%fused_computation.59 | convolution fusion | flops 1019584512 | bytes 7077888 | tf_op jit(solution)/shard_map/xyz,ky->xkz/dot_general | solution.py:52
  441.7 7.8 %fusion.12 = (f32[24,192,192]{2,1,0:T(8,128)}, f32[24,192,192]{2,1,0:T(8,128)}) fusion(f32[1,24,192,192]{3,2,1,0:T(8,128)S(1)} %bitcast.126, f32[]{:T(128)} %bitcast.25, f32[]{:T(128)} %bitcast.6, f32[192,24,192]{2,0,1:T(8,128)S(1)} %fusion.41), kind=kOutput, calls=%fused_computation.22 | convolution fusion | flops 1022238720 | bytes 14155784 | tf_op jit(solution)/shard_map/xyz,kz->xyk/dot_general | solution.py:48
  449.5 5.8 %reshape.207 = f32[6912,128]{1,0:T(8,128)} reshape(f32[24,192,192]{2,1,0:T(8,128)} %get-tuple-element.36) | data formatting | bytes 7077888 | tf_op jit(solution)/shard_map/reshape | solution.py:17
  475.2 13.8 %fusion.2 = f32[24,192,192]{2,1,0:T(8,128)} fusion(f32[192,24,192]{2,0,1:T(8,128)} %fusion.52, f32[24,192,192]{2,1,0:T(8,128)} %copy-done, f32[24,192,192]{2,1,0:T(8,128)} %copy-done.1, f32[24,192,192]{2,1,0:T(8,128)} %get-tuple-element.37, f32[]{:T(128)} %bitcast.19, f32[]{:T(128)} %bitcast.6, f32[]{:T(128)} %bitcast.1, f32[24,96,192]{2,1,0:T(8,128)S(1)} %fusion.36, ...), kind=kOutput, calls=%fused_computation.5 | convolution fusion | flops 515801088 | bytes 20152336 | tf_op jit(solution)/shard_map/xyz,ky->xkz/dot_general | solution.py:52
  489.0 45.6 %collective-permute-done.5 = f32[6912,128]{1,0:T(8,128)} collective-permute-done((f32[6912,128]{1,0:T(8,128)}, f32[6912,128]{1,0:T(8,128)}, u32[]{:S(2)}, u32[]{:S(2)}) %collective-permute-start.5) | collective-permute-done | bytes 3538976 | tf_op jit(solution)/shard_map/ppermute | solution.py:13
  534.6 5.0 reshape.208
  547.4 5.7 %fusion.34 = f32[192,24,192]{2,0,1:T(8,128)S(1)} fusion(f32[24,192,192]{2,1,0:T(8,128)} %reshape.206), kind=kOutput, calls=%fused_computation.52 | convolution fusion | flops 1019584512 | bytes 7077888 | tf_op jit(solution)/shard_map/xyz,ky->xkz/dot_general | solution.py:52
  553.1 5.0 fusion
  558.2 8.2 %negate_bitcast_fusion = f32[1,24,192,192]{3,2,1,0:T(8,128)} fusion(f32[24,192,192]{2,1,0:T(8,128)} %reshape.208, f32[24,192,192]{2,1,0:T(8,128)S(1)} %bitcast.130, f32[24,192,192]{2,1,0:T(8,128)} %fusion, f32[1,24,192,192]{3,2,1,0:T(8,128)S(1)} %bitcast.128, f32[]{:T(128)} %bitcast.25), kind=kLoop, calls=%fused_computation.12 | loop fusion | flops 4423680 | bytes 17694724 | tf_op jit(solution)/shard_map/neg | solution.py:204
  (121 shorter events, 145.0 us)
Async XLA Ops:
  2.9 27.2 %collective-permute-start = (f32[1728,128]{1,0:T(8,128)}, f32[1728,128]{1,0:T(8,128)}, u32[]{:S(2)}, u32[]{:S(2)}) collective-permute-start(f32[1728,128]{1,0:T(8,128)} %reshape.186), channel_id=1, source_target_pairs={{0,16},{8,0},{16,24},{24,8},{1,17},{9,1},{17,25},{25,9},{2,18},{10... | collective-permute-start | bytes 2654216 | tf_op jit(solution)/shard_map/ppermute | solution.py:13
  30.1 107.3 %all-to-all-start = ((f32[8,24,4608]{2,1,0:T(8,128)}), f32[8,24,4608]{2,1,0:T(8,128)}, u32[]{:S(2)}, u32[]{:S(2)}) async-start(f32[8,24,4608]{2,1,0:T(8,128)} %bitcast.119), calls=%async_computation | async-start | bytes 7077888 | tf_op jit(solution)/shard_map/all_to_all | solution.py:60
  39.9 60.7 %collective-permute-start.1 = (f32[5184,128]{1,0:T(8,128)}, f32[5184,128]{1,0:T(8,128)}, u32[]{:S(2)}, u32[]{:S(2)}) collective-permute-start(f32[5184,128]{1,0:T(8,128)} %reshape.187), channel_id=1, source_target_pairs={{0,16},{8,0},{16,24},{24,8},{1,17},{9,1},{17,25},{25,9},{2,18},{10... | collective-permute-start | bytes 7962632 | tf_op jit(solution)/shard_map/ppermute | solution.py:13
  102.1 9.4 %slice-start = ((s8[4718592]{0:T(1024)(128)(4,1)}), s8[524288]{0:T(1024)(128)(4,1)S(1)}, s32[]{:S(2)}) async-start(s8[4718592]{0:T(1024)(128)(4,1)} %bitcast.121), calls=%async_computation.6 | async-start | bytes 1048576
  114.8 22.6 %collective-permute-start.2 = (f32[1728,128]{1,0:T(8,128)}, f32[1728,128]{1,0:T(8,128)}, u32[]{:S(2)}, u32[]{:S(2)}) collective-permute-start(f32[1728,128]{1,0:T(8,128)} %reshape.186), channel_id=1, source_target_pairs={{0,24},{8,16},{16,8},{24,0},{1,25},{9,17},{17,9},{25,1},{2,26},{10... | collective-permute-start | bytes 2654216 | tf_op jit(solution)/shard_map/ppermute | solution.py:13
  137.4 5.0 copy-start.2
  137.4 92.3 %all-to-all-start.1 = ((f32[8,24,4608]{2,1,0:T(8,128)}), f32[8,24,4608]{2,1,0:T(8,128)}, u32[]{:S(2)}, u32[]{:S(2)}) async-start(f32[8,24,4608]{2,1,0:T(8,128)} %bitcast.118), calls=%async_computation.1 | async-start | bytes 7077888 | tf_op jit(solution)/shard_map/all_to_all | solution.py:60
  142.4 61.0 %collective-permute-start.3 = (f32[5184,128]{1,0:T(8,128)S(1)}, f32[5184,128]{1,0:T(8,128)}, u32[]{:S(2)}, u32[]{:S(2)}) collective-permute-start(f32[5184,128]{1,0:T(8,128)S(1)} %copy-done.2), channel_id=1, source_target_pairs={{0,24},{8,16},{16,8},{24,0},{1,25},{9,17},{17,9},{25,1},{2,26},{10... | collective-permute-start | bytes 7962632 | tf_op jit(solution)/shard_map/ppermute | solution.py:13
  204.8 9.4 %slice-start.2 = ((s8[4718592]{0:T(1024)(128)(4,1)}), s8[524288]{0:T(1024)(128)(4,1)S(1)}, s32[]{:S(2)}) async-start(s8[4718592]{0:T(1024)(128)(4,1)} %bitcast.123), calls=%async_computation.8 | async-start | bytes 1048576
  229.6 47.0 %all-to-all-start.2 = ((f32[8,24,2304]{2,1,0:T(8,128)}), f32[8,24,2304]{2,1,0:T(8,128)S(1)}, u32[]{:S(2)}, u32[]{:S(2)}) async-start(f32[8,24,2304]{2,1,0:T(8,128)} %bitcast.120), calls=%async_computation.2 | async-start | bytes 3538944 | tf_op jit(solution)/shard_map/all_to_all | solution.py:60
  283.1 45.6 %all-to-all-start.3 = ((f32[8,24,2304]{2,1,0:T(8,128)}), f32[8,24,2304]{2,1,0:T(8,128)S(1)}, u32[]{:S(2)}, u32[]{:S(2)}) async-start(f32[8,24,2304]{2,1,0:T(8,128)} %bitcast.134), calls=%async_computation.3 | async-start | bytes 3538944 | tf_op jit(solution)/shard_map/all_to_all | solution.py:60
  328.7 84.9 %all-to-all-start.4 = ((f32[8,24,4608]{2,1,0:T(8,128)}), f32[8,24,4608]{2,1,0:T(8,128)}, u32[]{:S(2)}, u32[]{:S(2)}) async-start(f32[8,24,4608]{2,1,0:T(8,128)} %bitcast.133), calls=%async_computation.4 | async-start | bytes 7077888 | tf_op jit(solution)/shard_map/all_to_all | solution.py:60
  342.3 82.4 %collective-permute-start.4 = (f32[3456,128]{1,0:T(8,128)}, f32[3456,128]{1,0:T(8,128)}, u32[]{:S(2)}, u32[]{:S(2)}) collective-permute-start(f32[3456,128]{1,0:T(8,128)} %reshape.199), channel_id=1, source_target_pairs={{0,24},{8,16},{16,8},{24,0},{1,25},{9,17},{17,9},{25,1},{2,26},{10... | collective-permute-start | bytes 5308424 | tf_op jit(solution)/shard_map/ppermute | solution.py:13
  413.6 6.7 %copy-start.5 = (s32[4]{0:T(128)S(1)}, s32[4]{0:T(128)}, u32[]{:S(2)}) copy-start(s32[4]{0:T(128)} %constant.94.clone) | copy-start | bytes 52
  413.6 8.5 %copy-start.3 = (s32[4]{0:T(128)S(1)}, s32[4]{0:T(128)}, u32[]{:S(2)}) copy-start(s32[4]{0:T(128)} %param.9) | copy-start | bytes 52
  413.6 8.5 %copy-start.4 = (f32[4]{0:T(128)S(1)}, f32[4]{0:T(128)}, u32[]{:S(2)}) copy-start(f32[4]{0:T(128)} %constant.93.clone) | copy-start | bytes 52
  413.6 126.1 %all-to-all-start.5 = ((f32[8,24,4608]{2,1,0:T(8,128)}), f32[8,24,4608]{2,1,0:T(8,128)}, u32[]{:S(2)}, u32[]{:S(2)}) async-start(f32[8,24,4608]{2,1,0:T(8,128)} %bitcast.132), calls=%async_computation.5 | async-start | bytes 7077888 | tf_op jit(solution)/shard_map/all_to_all | solution.py:60
  430.5 11.2 %slice-start.4 = ((s8[4718592]{0:T(1024)(128)(4,1)}), s8[524288]{0:T(1024)(128)(4,1)S(1)}, s32[]{:S(2)}) async-start(s8[4718592]{0:T(1024)(128)(4,1)} %bitcast.125), calls=%async_computation.10 | async-start | bytes 1048576
  436.0 5.7 %slice-start.5 = ((s8[4718592]{0:T(1024)(128)(4,1)}), s8[4194304]{0:T(1024)(128)(4,1)S(1)}, s32[]{:S(2)}) async-start(s8[4718592]{0:T(1024)(128)(4,1)} %bitcast.125), calls=%async_computation.11 | async-start | bytes 8388608
  455.3 79.4 %collective-permute-start.5 = (f32[6912,128]{1,0:T(8,128)}, f32[6912,128]{1,0:T(8,128)}, u32[]{:S(2)}, u32[]{:S(2)}) collective-permute-start(f32[6912,128]{1,0:T(8,128)} %reshape.207), channel_id=1, source_target_pairs={{0,8},{8,24},{16,0},{24,16},{1,9},{9,25},{17,1},{25,17},{2,10},{10... | collective-permute-start | bytes 10616840 | tf_op jit(solution)/shard_map/ppermute | solution.py:13
  547.4 10.8 %slice-start.6 = ((s8[4718592]{0:T(1024)(128)(4,1)}), s8[4194304]{0:T(1024)(128)(4,1)S(1)}, s32[]{:S(2)}) async-start(s8[4718592]{0:T(1024)(128)(4,1)} %bitcast.127), calls=%async_computation.12 | async-start | bytes 8388608
  547.4 10.8 %slice-start.9 = ((s8[4718592]{0:T(1024)(128)(4,1)}), s8[4194304]{0:T(1024)(128)(4,1)S(1)}, s32[]{:S(2)}) async-start(s8[4718592]{0:T(1024)(128)(4,1)} %bitcast.129), calls=%async_computation.15 | async-start | bytes 8388608
  553.1 5.1 slice-start.7
  553.1 5.1 slice-start.10
  (6 other events, 20.9 us)

commit v6 on v5

--- a/solution.py
+++ b/solution.py
@@ -149,7 +149,8 @@
         parts = lax.optimization_barrier(parts + earlier)[: len(parts)]
         return jnp.concatenate([part.reshape((-1,) + owned.shape[1:]) for part in parts])
 
-    blocks = after(forward(owned * owned), flat_guests[0][0])
+    density = after(owned, late_part)
+    blocks = after(forward(density * density), flat_guests[0][0])
     arrived = exchange(blocks)
     lines_self = arrived
     guests = []
@@ -178,6 +179,7 @@
     total = jnp.zeros_like(owned)
     away = []
     returned = []
+    cut = max(1, owned.shape[0] // 3)
     if shared:
         solved = solve_lines(half_lines, table, half_kernel, (place == 0) & (half == 0))
         half_back = exchange(after(solved, arrived))
@@ -185,12 +187,21 @@
         away.append(moved(flattened(half_back), "band", opposite))
         other_back = away[0].reshape(half_back.shape)
     for partners, guest, lines in zip(solo, guests, solo_lines):
+        own_scale = multiplicity(partners) * weight(groups)
+        guest_scale = multiplicity(partners) * weight(partners)
         solved = solve_lines(lines, table, kernel, place == 0)
-        arrived = exchange(after(solved, arrived))
-        field = multiplicity(partners) * backward(after(arrived, *away))
-        total = total + weight(partners) * guest * field
-        partial = flattened(weight(groups) * owned * field)
-        returned.append(moved(partial, "band", partners))
+        arrived = exchange(after(solved, arrived, own_scale, guest_scale))
+        earlier = away
+        fields = []
+        partials = []
+        for first, last in ((0, cut), (cut, owned.shape[0])):
+            field = backward(after(arrived, *earlier)[:, first:last])
+            partial = flattened(own_scale * owned[first:last] * field)
+            partials.append(moved(partial, "band", partners))
+            fields.append(field)
+            earlier = [partial]
+        total = total + guest_scale * guest * jnp.concatenate(fields)
+        returned.append(partials)
     if shared:
         own_part = along_y(along_z(from_blocks(half_back, half_rows), table), half_table.T)
         other_part = along_y(along_z(from_blocks(other_back, half_rows), table), other_table.T)
@@ -199,8 +210,10 @@
     solved = solve_lines(lines_self, table, kernel, place == 0)
     field = backward(exchange(after(solved, arrived)))
     total = after(total) + weight(groups) * owned * field
-    for partial in returned:
-        total = total + partial.reshape(owned.shape)
+    for partials in returned:
+        parts = lax.optimization_barrier((*partials, field))[: len(partials)]
+        parts = [part.reshape((-1,) + owned.shape[1:]) for part in parts]
+        total = total + jnp.concatenate(parts)
     return -total[None]
 
 

time: 576 us -> 558 us (0.969)
  waiting for transfers between devices: 297 us -> 277 us
    ppermute x6 -> x7, waiting for transfers between devices: 164 us -> 134 us  [moved(): return lax.ppermute(flat, axis, list(enumerate(targets)))]
    all_to_all x6, waiting for transfers between devices: 133 us -> 142 us  [exchange(): lax.all_to_all(blocks, 'space', split_axis=0, concat_axis=0, tiled=True)]
    dot_general x7 -> x8, matrix products: 30.7 us -> 36 us  [along_z(): return jnp.einsum('xyz,kz->xyk', field, table, precision=PRECISION)]
    dot_general x7 -> x8, matrix products: 46.4 us -> 41 us  [along_y(): return jnp.einsum('xyz,ky->xkz', field, table, precision=PRECISION)]
    ppermute x6 -> x7, starting transfers between devices: 10.6 us -> 13.8 us  [moved(): return lax.ppermute(flat, axis, list(enumerate(targets)))]
    reshape x4 -> x5, local copies, waits for them, and re-layouts: 14.3 us -> 12.8 us  [from_blocks(): return blocks.transpose(1, 0, 2).reshape(slab_rows, rows, -1)]
    reshape x4 -> x5, local copies, waits for them, and re-layouts: 11.6 us -> 10.3 us  [flattened(): return array.reshape(-1, 128)]
    transpose x4 -> x7, local copies, waits for them, and re-layouts: 13.5 us -> 14.3 us  [from_blocks(): return blocks.transpose(1, 0, 2).reshape(slab_rows, rows, -1)]
  transfers between devices with their start and end apart: 12 -> 13, of which waited for: 7 -> 7; matrix products, arithmetic and copies ran while one was open for 32% -> 34% of each run, Pallas kernels for 0% -> 0%
where the time goes in v6:
time: 558 us; the launch traced here: 548 us
  waiting for transfers between devices  277 us (50%)
  matrix products  102 us (18%)
  local copies, waits for them, and re-layouts  91.2 us (16%)
  starting transfers between devices  43 us (8%)
  other arithmetic  23.1 us (4%)
  between operations  12.4 us (2%)
    all_to_all x6, waiting for transfers between devices, exchange(): lax.all_to_all(blocks, 'space', split_axis=0, concat_axis=0, tiled=True)  142 us
    ppermute x7, waiting for transfers between devices, moved(): return lax.ppermute(flat, axis, list(enumerate(targets)))  134 us
    dot_general x8, matrix products, along_y(): return jnp.einsum('xyz,ky->xkz', field, table, precision=PRECISION)  41 us
    dot_general x8, matrix products, along_z(): return jnp.einsum('xyz,kz->xyk', field, table, precision=PRECISION)  36 us
    all_to_all x6, starting transfers between devices, exchange(): lax.all_to_all(blocks, 'space', split_axis=0, concat_axis=0, tiled=True)  29.2 us
    dot_general x6, matrix products, along_x(): return jnp.einsum('xn,kx->kn', lines, table, precision=PRECISION)  24.9 us
    reshape x6, local copies, waits for them, and re-layouts, to_blocks(): spectra.reshape(slab_rows, space_count, rows // space_count * length)  20.9 us
    transpose x7, local copies, waits for them, and re-layouts, from_blocks(): return blocks.transpose(1, 0, 2).reshape(slab_rows, rows, -1)  14.3 us
  transfers between devices with their start and end apart: 13, of which 7 were waited for; matrix products, arithmetic and copies ran while one was open for 34% of the time, Pallas kernels for 0%

profile of v6, /device:TPU:0, one launch (start us, length us, event | category | flops | bytes accessed | tf_op | source)
XLA Modules:
  0.0 548.3 jit_solution(13124985452423551481)
XLA Ops:
  14.3 5.3 fusion.9
  19.6 5.7 %add_bitcast_fusion.1 = f32[24,192,192]{2,1,0:T(8,128)} fusion(f32[192,192]{1,0:T(8,128)S(1)} %and_select_fusion.1, f32[24,192,192]{2,1,0:T(8,128)S(1)} %fusion.9), kind=kOutput, calls=%fused_computation.15 | convolution fusion | flops 1020469248 | bytes 7225344 | tf_op jit(solution)/shard_map/xyz,ky->xkz/dot_general | solution.py:52
  33.1 5.6 %all-to-all-start = ((f32[8,24,4608]{2,1,0:T(8,128)}), f32[8,24,4608]{2,1,0:T(8,128)}, u32[]{:S(2)}, u32[]{:S(2)}) async-start(f32[8,24,4608]{2,1,0:T(8,128)} %bitcast.128), calls=%async_computation | async-start | bytes 7077888 | tf_op jit(solution)/shard_map/all_to_all | solution.py:60
  40.5 58.5 %collective-permute-done.1 = f32[5184,128]{1,0:T(8,128)} collective-permute-done((f32[5184,128]{1,0:T(8,128)S(1)}, f32[5184,128]{1,0:T(8,128)}, u32[]{:S(2)}, u32[]{:S(2)}) %collective-permute-start.1) | collective-permute-done | bytes 2654240 | tf_op jit(solution)/shard_map/ppermute | solution.py:13
  115.7 6.7 %fusion.7 = f32[24,192,192]{2,1,0:T(8,128)S(1)} fusion(f32[]{:T(128)S(6)} %div.47, f32[24,192,192]{2,1,0:T(8,128)} %copy-done.1, f32[1,24,192,192]{3,2,1,0:T(8,128)} %param.9), kind=kOutput, calls=%fused_computation.13 | convolution fusion | flops 1021353984 | bytes 10616836 | tf_op jit(solution)/shard_map/xyz,kz->xyk/dot_general | solution.py:48
  122.4 5.7 %add_bitcast_fusion = f32[24,192,192]{2,1,0:T(8,128)} fusion(f32[192,192]{1,0:T(8,128)S(1)} %and_select_fusion, f32[24,192,192]{2,1,0:T(8,128)S(1)} %fusion.7), kind=kOutput, calls=%fused_computation.12 | convolution fusion | flops 1020469248 | bytes 7225344 | tf_op jit(solution)/shard_map/xyz,ky->xkz/dot_general | solution.py:52
  135.8 5.5 all-to-all-start.1
  144.1 58.3 %collective-permute-done.3 = f32[5184,128]{1,0:T(8,128)} collective-permute-done((f32[5184,128]{1,0:T(8,128)S(1)}, f32[5184,128]{1,0:T(8,128)}, u32[]{:S(2)}, u32[]{:S(2)}) %collective-permute-start.3) | collective-permute-done | bytes 2654240 | tf_op jit(solution)/shard_map/ppermute | solution.py:13
  215.7 5.3 fusion.5
  228.4 4.9 all-to-all-start.2
  233.6 41.7 %all-to-all-done.2 = f32[8,24,2304]{2,1,0:T(8,128)S(1)} async-done(((f32[8,24,2304]{2,1,0:T(8,128)}), f32[8,24,2304]{2,1,0:T(8,128)S(1)}, u32[]{:S(2)}, u32[]{:S(2)}) %all-to-all-start.2) | async-done | bytes 1769504 | tf_op jit(solution)/shard_map/all_to_all | solution.py:60
  299.2 5.5 %convolution_multiply_fusion.1 = f32[192,4608]{1,0:T(8,128)S(1)} fusion(f32[192,4608]{1,0:T(8,128)} %bitcast.8, s32[4608]{0:T(1024)S(1)} %mul.273, s32[4608]{0:T(1024)S(1)} %mul.272, s32[192]{0:T(256)S(1)} %fusion.70, f32[4608]{0:T(1024)S(1)} %get-tuple-element.49), kind=kOutput, calls=%fused_computation.1 | convolution fusion | flops 1029316608 | bytes 7133952 | tf_op jit(solution)/shard_map/xn,kx->kn/dot_general | solution.py:56
  309.1 18.3 %all-to-all-done.3 = f32[8,24,2304]{2,1,0:T(8,128)S(1)} async-done(((f32[8,24,2304]{2,1,0:T(8,128)}), f32[8,24,2304]{2,1,0:T(8,128)S(1)}, u32[]{:S(2)}, u32[]{:S(2)}) %all-to-all-start.3) | async-done | bytes 1769504 | tf_op jit(solution)/shard_map/all_to_all | solution.py:60
  335.3 5.5 %convolution_multiply_fusion = f32[192,4608]{1,0:T(8,128)S(1)} fusion(f32[192,4608]{1,0:T(8,128)} %bitcast.29, f32[4608]{0:T(1024)S(1)} %get-tuple-element.48, s32[4608]{0:T(1024)S(1)} %mul.273, s32[4608]{0:T(1024)S(1)} %mul.272, s32[192]{0:T(256)S(1)} %fusion.70), kind=kOutput, calls=%fused_computation | convolution fusion | flops 1029316608 | bytes 7133952 | tf_op jit(solution)/shard_map/xn,kx->kn/dot_general | solution.py:56
  345.3 66.7 %all-to-all-done.4 = f32[8,24,4608]{2,1,0:T(8,128)} async-done(((f32[8,24,4608]{2,1,0:T(8,128)}), f32[8,24,4608]{2,1,0:T(8,128)}, u32[]{:S(2)}, u32[]{:S(2)}) %all-to-all-start.4) | async-done | bytes 3538976 | tf_op jit(solution)/shard_map/all_to_all | solution.py:60
  412.0 4.9 all-to-all-start.5
  444.8 5.8 %bitcast_multiply_fusion.1 = (f32[16,192,192]{2,1,0:T(8,128)S(1)}, f32[16,192,192]{2,1,0:T(8,128)}) fusion(f32[1,24,192,192]{3,2,1,0:T(8,128)} %param.9, f32[]{:T(128)} %bitcast.15, f32[192,16,192]{2,0,1:T(8,128)S(1)} %fusion.42), kind=kOutput, calls=%fused_computation.28 | convolution fusion | flops 681025536 | bytes 9437188 | tf_op jit(solution)/shard_map/xyz,kz->xyk/dot_general | solution.py:48
  454.1 5.9 %fusion.56 = f32[192,24,192]{2,0,1:T(8,128)} fusion(f32[24,96,192]{2,1,0:T(8,128)} %fusion.39, f32[192,192]{1,0:T(8,128)S(1)} %sine_add_fusion, s32[]{:T(128)S(6)} %select_n.152), kind=kOutput, calls=%fused_computation.81 | convolution fusion | flops 509607936 | bytes 5406724 | tf_op jit(solution)/shard_map/xyz,ky->xkz/dot_general | solution.py:52
  472.5 8.8 %fusion = f32[24,192,192]{2,1,0:T(8,128)} fusion(f32[16,192,192]{2,1,0:T(8,128)S(1)} %copy-done.2, f32[8,192,192]{2,1,0:T(8,128)S(1)} %copy-done.3, f32[192,24,192]{2,0,1:T(8,128)} %fusion.56, f32[24,192,192]{2,1,0:T(8,128)} %copy-done, f32[24,192,192]{2,1,0:T(8,128)} %copy-done.1, f32[]{:T(128)} %bitcast.22, f32[]{:T(128)} %bitcast.1, ...), kind=kOutput, calls=%fused_computation.3 | convolution fusion | flops 515801088 | bytes 21331980 | tf_op jit(solution)/shard_map/xyz,ky->xkz/dot_general | solution.py:52
  481.3 15.5 %all-to-all-done.5 = f32[8,24,4608]{2,1,0:T(8,128)} async-done(((f32[8,24,4608]{2,1,0:T(8,128)}), f32[8,24,4608]{2,1,0:T(8,128)}, u32[]{:S(2)}, u32[]{:S(2)}) %all-to-all-start.5) | async-done | bytes 3538976 | tf_op jit(solution)/shard_map/all_to_all | solution.py:60
  504.3 5.5 %fusion.35 = f32[192,24,192]{2,0,1:T(8,128)S(1)} fusion(f32[24,192,192]{2,1,0:T(8,128)} %reshape.225), kind=kOutput, calls=%fused_computation.55 | convolution fusion | flops 1019584512 | bytes 7077888 | tf_op jit(solution)/shard_map/xyz,ky->xkz/dot_general | solution.py:52
  509.8 5.0 fusion.3
  514.9 17.6 %collective-permute-done.5 = f32[2304,128]{1,0:T(8,128)} collective-permute-done((f32[2304,128]{1,0:T(8,128)}, f32[2304,128]{1,0:T(8,128)}, u32[]{:S(2)}, u32[]{:S(2)}) %collective-permute-start.5) | collective-permute-done | bytes 1179680 | tf_op jit(solution)/shard_map/ppermute | solution.py:13
  537.8 10.2 %fusion.2 = f32[1,24,192,192]{3,2,1,0:T(8,128)} fusion(f32[16,192,192]{2,1,0:T(8,128)S(1)} %reshape.228, f32[8,192,192]{2,1,0:T(8,128)} %reshape.227, f32[24,192,192]{2,1,0:T(8,128)} %fusion, f32[24,192,192]{2,1,0:T(8,128)} %fusion.3, f32[]{:T(128)} %bitcast.28, f32[1,24,192,192]{3,2,1,0:T(8,128)} %param.9), kind=kLoop, calls=%fused_computation.6 | loop fusion | flops 5308416 | bytes 17694724 | tf_op jit(solution)/shard_map/neg | solution.py:217
  (122 shorter events, 157.3 us)
Async XLA Ops:
  2.9 30.2 %collective-permute-start = (f32[1728,128]{1,0:T(8,128)}, f32[1728,128]{1,0:T(8,128)}, u32[]{:S(2)}, u32[]{:S(2)}) collective-permute-start(f32[1728,128]{1,0:T(8,128)} %reshape.203), channel_id=1, source_target_pairs={{0,16},{8,0},{16,24},{24,8},{1,17},{9,1},{17,25},{25,9},{2,18},{10... | collective-permute-start | bytes 2654216 | tf_op jit(solution)/shard_map/ppermute | solution.py:13
  33.1 5.6 %copy-start.4 = (f32[5184,128]{1,0:T(8,128)S(1)}, f32[5184,128]{1,0:T(8,128)}, u32[]{:S(2)}) copy-start(f32[5184,128]{1,0:T(8,128)} %reshape.204) | copy-start | bytes 7962628
  33.1 102.7 %all-to-all-start = ((f32[8,24,4608]{2,1,0:T(8,128)}), f32[8,24,4608]{2,1,0:T(8,128)}, u32[]{:S(2)}, u32[]{:S(2)}) async-start(f32[8,24,4608]{2,1,0:T(8,128)} %bitcast.128), calls=%async_computation | async-start | bytes 7077888 | tf_op jit(solution)/shard_map/all_to_all | solution.py:60
  38.7 60.3 %collective-permute-start.1 = (f32[5184,128]{1,0:T(8,128)S(1)}, f32[5184,128]{1,0:T(8,128)}, u32[]{:S(2)}, u32[]{:S(2)}) collective-permute-start(f32[5184,128]{1,0:T(8,128)S(1)} %copy-done.4), channel_id=1, source_target_pairs={{0,16},{8,0},{16,24},{24,8},{1,17},{9,1},{17,25},{25,9},{2,18},{10... | collective-permute-start | bytes 7962632 | tf_op jit(solution)/shard_map/ppermute | solution.py:13
  100.4 9.4 %slice-start = ((s8[4718592]{0:T(1024)(128)(4,1)}), s8[524288]{0:T(1024)(128)(4,1)S(1)}, s32[]{:S(2)}) async-start(s8[4718592]{0:T(1024)(128)(4,1)} %bitcast.132), calls=%async_computation.6 | async-start | bytes 1048576
  105.0 4.9 slice-start.1
  113.0 22.7 %collective-permute-start.2 = (f32[1728,128]{1,0:T(8,128)}, f32[1728,128]{1,0:T(8,128)}, u32[]{:S(2)}, u32[]{:S(2)}) collective-permute-start(f32[1728,128]{1,0:T(8,128)} %reshape.203), channel_id=1, source_target_pairs={{0,24},{8,16},{16,8},{24,0},{1,25},{9,17},{17,9},{25,1},{2,26},{10... | collective-permute-start | bytes 2654216 | tf_op jit(solution)/shard_map/ppermute | solution.py:13
  135.8 5.5 copy-start.5
  135.8 92.6 %all-to-all-start.1 = ((f32[8,24,4608]{2,1,0:T(8,128)}), f32[8,24,4608]{2,1,0:T(8,128)}, u32[]{:S(2)}, u32[]{:S(2)}) async-start(f32[8,24,4608]{2,1,0:T(8,128)} %bitcast.127), calls=%async_computation.1 | async-start | bytes 7077888 | tf_op jit(solution)/shard_map/all_to_all | solution.py:60
  141.3 61.0 %collective-permute-start.3 = (f32[5184,128]{1,0:T(8,128)S(1)}, f32[5184,128]{1,0:T(8,128)}, u32[]{:S(2)}, u32[]{:S(2)}) collective-permute-start(f32[5184,128]{1,0:T(8,128)S(1)} %copy-done.5), channel_id=1, source_target_pairs={{0,24},{8,16},{16,8},{24,0},{1,25},{9,17},{17,9},{25,1},{2,26},{10... | collective-permute-start | bytes 7962632 | tf_op jit(solution)/shard_map/ppermute | solution.py:13
  203.8 9.4 %slice-start.2 = ((s8[4718592]{0:T(1024)(128)(4,1)}), s8[524288]{0:T(1024)(128)(4,1)S(1)}, s32[]{:S(2)}) async-start(s8[4718592]{0:T(1024)(128)(4,1)} %bitcast.134), calls=%async_computation.8 | async-start | bytes 1048576
  228.4 47.0 %all-to-all-start.2 = ((f32[8,24,2304]{2,1,0:T(8,128)}), f32[8,24,2304]{2,1,0:T(8,128)S(1)}, u32[]{:S(2)}, u32[]{:S(2)}) async-start(f32[8,24,2304]{2,1,0:T(8,128)} %bitcast.129), calls=%async_computation.2 | async-start | bytes 3538944 | tf_op jit(solution)/shard_map/all_to_all | solution.py:60
  278.8 6.6 %copy-start.9 = (s32[4]{0:T(128)S(1)}, s32[4]{0:T(128)}, u32[]{:S(2)}) copy-start(s32[4]{0:T(128)} %constant.96.clone) | copy-start | bytes 52
  278.9 8.5 %copy-start.8 = (s32[4]{0:T(128)S(1)}, s32[4]{0:T(128)}, u32[]{:S(2)}) copy-start(s32[4]{0:T(128)} %constant.94.clone) | copy-start | bytes 52
  278.9 10.5 %copy-start.7 = (f32[4]{0:T(128)S(1)}, f32[4]{0:T(128)}, u32[]{:S(2)}) copy-start(f32[4]{0:T(128)} %constant.93.clone) | copy-start | bytes 52
  278.9 11.1 %copy-start.6 = (s32[4]{0:T(128)S(1)}, s32[4]{0:T(128)}, u32[]{:S(2)}) copy-start(s32[4]{0:T(128)} %param.10) | copy-start | bytes 52
  281.8 45.6 %all-to-all-start.3 = ((f32[8,24,2304]{2,1,0:T(8,128)}), f32[8,24,2304]{2,1,0:T(8,128)S(1)}, u32[]{:S(2)}, u32[]{:S(2)}) async-start(f32[8,24,2304]{2,1,0:T(8,128)} %bitcast.14), calls=%async_computation.3 | async-start | bytes 3538944 | tf_op jit(solution)/shard_map/all_to_all | solution.py:60
  327.4 84.7 %all-to-all-start.4 = ((f32[8,24,4608]{2,1,0:T(8,128)}), f32[8,24,4608]{2,1,0:T(8,128)}, u32[]{:S(2)}, u32[]{:S(2)}) async-start(f32[8,24,4608]{2,1,0:T(8,128)} %bitcast.138), calls=%async_computation.4 | async-start | bytes 7077888 | tf_op jit(solution)/shard_map/all_to_all | solution.py:60
  333.4 91.3 %collective-permute-start.4 = (f32[3456,128]{1,0:T(8,128)}, f32[3456,128]{1,0:T(8,128)}, u32[]{:S(2)}, u32[]{:S(2)}) collective-permute-start(f32[3456,128]{1,0:T(8,128)} %reshape.216), channel_id=1, source_target_pairs={{0,24},{8,16},{16,8},{24,0},{1,25},{9,17},{17,9},{25,1},{2,26},{10... | collective-permute-start | bytes 5308424 | tf_op jit(solution)/shard_map/ppermute | solution.py:13
  412.0 84.9 %all-to-all-start.5 = ((f32[8,24,4608]{2,1,0:T(8,128)}), f32[8,24,4608]{2,1,0:T(8,128)}, u32[]{:S(2)}, u32[]{:S(2)}) async-start(f32[8,24,4608]{2,1,0:T(8,128)} %bitcast.137), calls=%async_computation.5 | async-start | bytes 7077888 | tf_op jit(solution)/shard_map/all_to_all | solution.py:60
  453.2 79.2 %collective-permute-start.6 = (f32[4608,128]{1,0:T(8,128)}, f32[4608,128]{1,0:T(8,128)}, u32[]{:S(2)}, u32[]{:S(2)}) collective-permute-start(f32[4608,128]{1,0:T(8,128)} %reshape.226), channel_id=1, source_target_pairs={{0,8},{8,24},{16,0},{24,16},{1,9},{9,25},{17,1},{25,17},{2,10},{10... | collective-permute-start | bytes 7077896 | tf_op jit(solution)/shard_map/ppermute | solution.py:13
  463.4 9.1 %copy-start.2 = (f32[16,192,192]{2,1,0:T(8,128)S(1)}, f32[16,192,192]{2,1,0:T(8,128)}, u32[]{:S(2)}) copy-start(f32[16,192,192]{2,1,0:T(8,128)} %get-tuple-element.47) | copy-start | bytes 7077892
  467.0 5.5 %copy-start.3 = (f32[8,192,192]{2,1,0:T(8,128)S(1)}, f32[8,192,192]{2,1,0:T(8,128)}, u32[]{:S(2)}) copy-start(f32[8,192,192]{2,1,0:T(8,128)} %get-tuple-element.45) | copy-start | bytes 3538948
  470.7 61.7 %collective-permute-start.5 = (f32[2304,128]{1,0:T(8,128)}, f32[2304,128]{1,0:T(8,128)}, u32[]{:S(2)}, u32[]{:S(2)}) collective-permute-start(f32[2304,128]{1,0:T(8,128)} %reshape.218), channel_id=1, source_target_pairs={{0,8},{8,24},{16,0},{24,16},{1,9},{9,25},{17,1},{25,17},{2,10},{10... | collective-permute-start | bytes 3538952 | tf_op jit(solution)/shard_map/ppermute | solution.py:13
  (4 other events, 12.2 us)

commit v7 on v6

--- a/solution.py
+++ b/solution.py
@@ -197,7 +197,7 @@
         for first, last in ((0, cut), (cut, owned.shape[0])):
             field = backward(after(arrived, *earlier)[:, first:last])
             partial = flattened(own_scale * owned[first:last] * field)
-            partials.append(moved(partial, "band", partners))
+            partials.append(moved(after(partial, *partials), "band", partners))
             fields.append(field)
             earlier = [partial]
         total = total + guest_scale * guest * jnp.concatenate(fields)

time: 558 us -> 542 us (0.971)
  waiting for transfers between devices: 277 us -> 262 us
    all_to_all x6, waiting for transfers between devices: 142 us -> 133 us  [exchange(): lax.all_to_all(blocks, 'space', split_axis=0, concat_axis=0, tiled=True)]
    ppermute x7, waiting for transfers between devices: 134 us -> 128 us  [moved(): return lax.ppermute(flat, axis, list(enumerate(targets)))]
  transfers between devices with their start and end apart: 13 -> 13, of which waited for: 7 -> 8; matrix products, arithmetic and copies ran while one was open for 34% -> 35% of each run, Pallas kernels for 0% -> 0%
where the time goes in v7:
time: 542 us; the launch traced here: 533 us
  waiting for transfers between devices  262 us (48%)
  matrix products  102 us (19%)
  local copies, waits for them, and re-layouts  91.3 us (17%)
  starting transfers between devices  42.6 us (8%)
  other arithmetic  23.1 us (4%)
  between operations  12.4 us (2%)
    all_to_all x6, waiting for transfers between devices, exchange(): lax.all_to_all(blocks, 'space', split_axis=0, concat_axis=0, tiled=True)  133 us
    ppermute x7, waiting for transfers between devices, moved(): return lax.ppermute(flat, axis, list(enumerate(targets)))  128 us
    dot_general x8, matrix products, along_y(): return jnp.einsum('xyz,ky->xkz', field, table, precision=PRECISION)  41 us
    dot_general x8, matrix products, along_z(): return jnp.einsum('xyz,kz->xyk', field, table, precision=PRECISION)  36 us
    all_to_all x6, starting transfers between devices, exchange(): lax.all_to_all(blocks, 'space', split_axis=0, concat_axis=0, tiled=True)  29.1 us
    dot_general x6, matrix products, along_x(): return jnp.einsum('xn,kx->kn', lines, table, precision=PRECISION)  24.9 us
    reshape x6, local copies, waits for them, and re-layouts, to_blocks(): spectra.reshape(slab_rows, space_count, rows // space_count * length)  20.9 us
    transpose x7, local copies, waits for them, and re-layouts, from_blocks(): return blocks.transpose(1, 0, 2).reshape(slab_rows, rows, -1)  14.3 us
  transfers between devices with their start and end apart: 13, of which 8 were waited for; matrix products, arithmetic and copies ran while one was open for 35% of the time, Pallas kernels for 0%

profile of v7, /device:TPU:0, one launch (start us, length us, event | category | flops | bytes accessed | tf_op | source)
XLA Modules:
  0.0 533.1 jit_solution(8563716312088413094)
XLA Ops:
  14.3 5.3 fusion.9
  19.6 5.7 %add_bitcast_fusion.1 = f32[24,192,192]{2,1,0:T(8,128)} fusion(f32[192,192]{1,0:T(8,128)S(1)} %and_select_fusion.1, f32[24,192,192]{2,1,0:T(8,128)S(1)} %fusion.9), kind=kOutput, calls=%fused_computation.15 | convolution fusion | flops 1020469248 | bytes 7225344 | tf_op jit(solution)/shard_map/xyz,ky->xkz/dot_general | solution.py:52
  33.1 5.6 %all-to-all-start = ((f32[8,24,4608]{2,1,0:T(8,128)}), f32[8,24,4608]{2,1,0:T(8,128)}, u32[]{:S(2)}, u32[]{:S(2)}) async-start(f32[8,24,4608]{2,1,0:T(8,128)} %bitcast.128), calls=%async_computation | async-start | bytes 7077888 | tf_op jit(solution)/shard_map/all_to_all | solution.py:60
  40.7 58.5 %collective-permute-done.1 = f32[5184,128]{1,0:T(8,128)} collective-permute-done((f32[5184,128]{1,0:T(8,128)S(1)}, f32[5184,128]{1,0:T(8,128)}, u32[]{:S(2)}, u32[]{:S(2)}) %collective-permute-start.1) | collective-permute-done | bytes 2654240 | tf_op jit(solution)/shard_map/ppermute | solution.py:13
  115.9 6.7 %fusion.7 = f32[24,192,192]{2,1,0:T(8,128)S(1)} fusion(f32[]{:T(128)S(6)} %div.47, f32[24,192,192]{2,1,0:T(8,128)} %copy-done.1, f32[1,24,192,192]{3,2,1,0:T(8,128)} %param.9), kind=kOutput, calls=%fused_computation.13 | convolution fusion | flops 1021353984 | bytes 10616836 | tf_op jit(solution)/shard_map/xyz,kz->xyk/dot_general | solution.py:48
  122.6 5.7 %add_bitcast_fusion = f32[24,192,192]{2,1,0:T(8,128)} fusion(f32[192,192]{1,0:T(8,128)S(1)} %and_select_fusion, f32[24,192,192]{2,1,0:T(8,128)S(1)} %fusion.7), kind=kOutput, calls=%fused_computation.12 | convolution fusion | flops 1020469248 | bytes 7225344 | tf_op jit(solution)/shard_map/xyz,ky->xkz/dot_general | solution.py:52
  136.1 5.2 all-to-all-start.1
  144.1 58.3 %collective-permute-done.3 = f32[5184,128]{1,0:T(8,128)} collective-permute-done((f32[5184,128]{1,0:T(8,128)S(1)}, f32[5184,128]{1,0:T(8,128)}, u32[]{:S(2)}, u32[]{:S(2)}) %collective-permute-start.3) | collective-permute-done | bytes 2654240 | tf_op jit(solution)/shard_map/ppermute | solution.py:13
  215.7 5.3 fusion.5
  228.4 5.0 all-to-all-start.2
  233.7 41.7 %all-to-all-done.2 = f32[8,24,2304]{2,1,0:T(8,128)S(1)} async-done(((f32[8,24,2304]{2,1,0:T(8,128)}), f32[8,24,2304]{2,1,0:T(8,128)S(1)}, u32[]{:S(2)}, u32[]{:S(2)}) %all-to-all-start.2) | async-done | bytes 1769504 | tf_op jit(solution)/shard_map/all_to_all | solution.py:60
  299.2 5.5 %convolution_multiply_fusion.1 = f32[192,4608]{1,0:T(8,128)S(1)} fusion(f32[192,4608]{1,0:T(8,128)} %bitcast.8, s32[4608]{0:T(1024)S(1)} %mul.273, s32[4608]{0:T(1024)S(1)} %mul.272, s32[192]{0:T(256)S(1)} %fusion.70, f32[4608]{0:T(1024)S(1)} %get-tuple-element.51), kind=kOutput, calls=%fused_computation.1 | convolution fusion | flops 1029316608 | bytes 7133952 | tf_op jit(solution)/shard_map/xn,kx->kn/dot_general | solution.py:56
  309.1 18.3 %all-to-all-done.3 = f32[8,24,2304]{2,1,0:T(8,128)S(1)} async-done(((f32[8,24,2304]{2,1,0:T(8,128)}), f32[8,24,2304]{2,1,0:T(8,128)S(1)}, u32[]{:S(2)}, u32[]{:S(2)}) %all-to-all-start.3) | async-done | bytes 1769504 | tf_op jit(solution)/shard_map/all_to_all | solution.py:60
  335.4 5.5 %convolution_multiply_fusion = f32[192,4608]{1,0:T(8,128)S(1)} fusion(f32[192,4608]{1,0:T(8,128)} %bitcast.29, f32[4608]{0:T(1024)S(1)} %get-tuple-element.50, s32[4608]{0:T(1024)S(1)} %mul.273, s32[4608]{0:T(1024)S(1)} %mul.272, s32[192]{0:T(256)S(1)} %fusion.70), kind=kOutput, calls=%fused_computation | convolution fusion | flops 1029316608 | bytes 7133952 | tf_op jit(solution)/shard_map/xn,kx->kn/dot_general | solution.py:56
  345.4 66.7 %all-to-all-done.4 = f32[8,24,4608]{2,1,0:T(8,128)} async-done(((f32[8,24,4608]{2,1,0:T(8,128)}), f32[8,24,4608]{2,1,0:T(8,128)}, u32[]{:S(2)}, u32[]{:S(2)}) %all-to-all-start.4) | async-done | bytes 3538976 | tf_op jit(solution)/shard_map/all_to_all | solution.py:60
  412.1 5.0 all-to-all-start.5
  445.9 5.8 %bitcast_multiply_fusion.1 = (f32[16,192,192]{2,1,0:T(8,128)S(1)}, f32[16,192,192]{2,1,0:T(8,128)}) fusion(f32[1,24,192,192]{3,2,1,0:T(8,128)} %param.9, f32[]{:T(128)} %bitcast.15, f32[192,16,192]{2,0,1:T(8,128)S(1)} %fusion.42), kind=kOutput, calls=%fused_computation.28 | convolution fusion | flops 681025536 | bytes 9437188 | tf_op jit(solution)/shard_map/xyz,kz->xyk/dot_general | solution.py:48
  454.3 9.5 %collective-permute-done.5 = f32[2304,128]{1,0:T(8,128)} collective-permute-done((f32[2304,128]{1,0:T(8,128)}, f32[2304,128]{1,0:T(8,128)}, u32[]{:S(2)}, u32[]{:S(2)}) %collective-permute-start.5) | collective-permute-done | bytes 1179680 | tf_op jit(solution)/shard_map/ppermute | solution.py:13
  465.0 5.9 %fusion.56 = f32[192,24,192]{2,0,1:T(8,128)} fusion(f32[24,96,192]{2,1,0:T(8,128)} %fusion.39, f32[192,192]{1,0:T(8,128)S(1)} %sine_add_fusion, s32[]{:T(128)S(6)} %select_n.152), kind=kOutput, calls=%fused_computation.81 | convolution fusion | flops 509607936 | bytes 5406724 | tf_op jit(solution)/shard_map/xyz,ky->xkz/dot_general | solution.py:52
  481.6 8.8 %fusion = f32[24,192,192]{2,1,0:T(8,128)} fusion(f32[16,192,192]{2,1,0:T(8,128)S(1)} %copy-done.2, f32[8,192,192]{2,1,0:T(8,128)S(1)} %copy-done.3, f32[192,24,192]{2,0,1:T(8,128)} %fusion.56, f32[24,192,192]{2,1,0:T(8,128)} %copy-done, f32[24,192,192]{2,1,0:T(8,128)} %copy-done.1, f32[]{:T(128)} %bitcast.22, f32[]{:T(128)} %bitcast.1, ...), kind=kOutput, calls=%fused_computation.3 | convolution fusion | flops 515801088 | bytes 21331980 | tf_op jit(solution)/shard_map/xyz,ky->xkz/dot_general | solution.py:52
  490.4 6.6 %all-to-all-done.5 = f32[8,24,4608]{2,1,0:T(8,128)} async-done(((f32[8,24,4608]{2,1,0:T(8,128)}), f32[8,24,4608]{2,1,0:T(8,128)}, u32[]{:S(2)}, u32[]{:S(2)}) %all-to-all-start.5) | async-done | bytes 3538976 | tf_op jit(solution)/shard_map/all_to_all | solution.py:60
  504.7 5.6 %fusion.35 = f32[192,24,192]{2,0,1:T(8,128)S(1)} fusion(f32[24,192,192]{2,1,0:T(8,128)} %reshape.225), kind=kOutput, calls=%fused_computation.55 | convolution fusion | flops 1019584512 | bytes 7077888 | tf_op jit(solution)/shard_map/xyz,ky->xkz/dot_general | solution.py:52
  510.2 5.0 fusion.3
  522.5 10.2 %fusion.2 = f32[1,24,192,192]{3,2,1,0:T(8,128)} fusion(f32[16,192,192]{2,1,0:T(8,128)S(1)} %reshape.228, f32[8,192,192]{2,1,0:T(8,128)} %reshape.227, f32[24,192,192]{2,1,0:T(8,128)} %fusion, f32[24,192,192]{2,1,0:T(8,128)} %fusion.3, f32[]{:T(128)} %bitcast.28, f32[1,24,192,192]{3,2,1,0:T(8,128)} %param.9), kind=kLoop, calls=%fused_computation.6 | loop fusion | flops 5308416 | bytes 17694724 | tf_op jit(solution)/shard_map/neg | solution.py:217
  (122 shorter events, 159.2 us)
Async XLA Ops:
  2.9 30.2 %collective-permute-start = (f32[1728,128]{1,0:T(8,128)}, f32[1728,128]{1,0:T(8,128)}, u32[]{:S(2)}, u32[]{:S(2)}) collective-permute-start(f32[1728,128]{1,0:T(8,128)} %reshape.203), channel_id=1, source_target_pairs={{0,16},{8,0},{16,24},{24,8},{1,17},{9,1},{17,25},{25,9},{2,18},{10... | collective-permute-start | bytes 2654216 | tf_op jit(solution)/shard_map/ppermute | solution.py:13
  33.1 5.6 %copy-start.4 = (f32[5184,128]{1,0:T(8,128)S(1)}, f32[5184,128]{1,0:T(8,128)}, u32[]{:S(2)}) copy-start(f32[5184,128]{1,0:T(8,128)} %reshape.204) | copy-start | bytes 7962628
  33.1 103.0 %all-to-all-start = ((f32[8,24,4608]{2,1,0:T(8,128)}), f32[8,24,4608]{2,1,0:T(8,128)}, u32[]{:S(2)}, u32[]{:S(2)}) async-start(f32[8,24,4608]{2,1,0:T(8,128)} %bitcast.128), calls=%async_computation | async-start | bytes 7077888 | tf_op jit(solution)/shard_map/all_to_all | solution.py:60
  38.7 60.5 %collective-permute-start.1 = (f32[5184,128]{1,0:T(8,128)S(1)}, f32[5184,128]{1,0:T(8,128)}, u32[]{:S(2)}, u32[]{:S(2)}) collective-permute-start(f32[5184,128]{1,0:T(8,128)S(1)} %copy-done.4), channel_id=1, source_target_pairs={{0,16},{8,0},{16,24},{24,8},{1,17},{9,1},{17,25},{25,9},{2,18},{10... | collective-permute-start | bytes 7962632 | tf_op jit(solution)/shard_map/ppermute | solution.py:13
  100.7 9.4 %slice-start = ((s8[4718592]{0:T(1024)(128)(4,1)}), s8[524288]{0:T(1024)(128)(4,1)S(1)}, s32[]{:S(2)}) async-start(s8[4718592]{0:T(1024)(128)(4,1)} %bitcast.132), calls=%async_computation.6 | async-start | bytes 1048576
  105.2 4.9 slice-start.1
  113.3 22.7 %collective-permute-start.2 = (f32[1728,128]{1,0:T(8,128)}, f32[1728,128]{1,0:T(8,128)}, u32[]{:S(2)}, u32[]{:S(2)}) collective-permute-start(f32[1728,128]{1,0:T(8,128)} %reshape.203), channel_id=1, source_target_pairs={{0,24},{8,16},{16,8},{24,0},{1,25},{9,17},{17,9},{25,1},{2,26},{10... | collective-permute-start | bytes 2654216 | tf_op jit(solution)/shard_map/ppermute | solution.py:13
  136.0 5.2 copy-start.5
  136.1 92.4 %all-to-all-start.1 = ((f32[8,24,4608]{2,1,0:T(8,128)}), f32[8,24,4608]{2,1,0:T(8,128)}, u32[]{:S(2)}, u32[]{:S(2)}) async-start(f32[8,24,4608]{2,1,0:T(8,128)} %bitcast.127), calls=%async_computation.1 | async-start | bytes 7077888 | tf_op jit(solution)/shard_map/all_to_all | solution.py:60
  141.3 61.0 %collective-permute-start.3 = (f32[5184,128]{1,0:T(8,128)S(1)}, f32[5184,128]{1,0:T(8,128)}, u32[]{:S(2)}, u32[]{:S(2)}) collective-permute-start(f32[5184,128]{1,0:T(8,128)S(1)} %copy-done.5), channel_id=1, source_target_pairs={{0,24},{8,16},{16,8},{24,0},{1,25},{9,17},{17,9},{25,1},{2,26},{10... | collective-permute-start | bytes 7962632 | tf_op jit(solution)/shard_map/ppermute | solution.py:13
  203.8 9.4 %slice-start.2 = ((s8[4718592]{0:T(1024)(128)(4,1)}), s8[524288]{0:T(1024)(128)(4,1)S(1)}, s32[]{:S(2)}) async-start(s8[4718592]{0:T(1024)(128)(4,1)} %bitcast.134), calls=%async_computation.8 | async-start | bytes 1048576
  208.3 4.8 slice-start.3
  228.4 47.0 %all-to-all-start.2 = ((f32[8,24,2304]{2,1,0:T(8,128)}), f32[8,24,2304]{2,1,0:T(8,128)S(1)}, u32[]{:S(2)}, u32[]{:S(2)}) async-start(f32[8,24,2304]{2,1,0:T(8,128)} %bitcast.129), calls=%async_computation.2 | async-start | bytes 3538944 | tf_op jit(solution)/shard_map/all_to_all | solution.py:60
  278.9 6.6 %copy-start.9 = (s32[4]{0:T(128)S(1)}, s32[4]{0:T(128)}, u32[]{:S(2)}) copy-start(s32[4]{0:T(128)} %constant.96.clone) | copy-start | bytes 52
  278.9 8.5 %copy-start.8 = (s32[4]{0:T(128)S(1)}, s32[4]{0:T(128)}, u32[]{:S(2)}) copy-start(s32[4]{0:T(128)} %constant.94.clone) | copy-start | bytes 52
  278.9 10.5 %copy-start.7 = (f32[4]{0:T(128)S(1)}, f32[4]{0:T(128)}, u32[]{:S(2)}) copy-start(f32[4]{0:T(128)} %constant.93.clone) | copy-start | bytes 52
  278.9 11.1 %copy-start.6 = (s32[4]{0:T(128)S(1)}, s32[4]{0:T(128)}, u32[]{:S(2)}) copy-start(s32[4]{0:T(128)} %param.10) | copy-start | bytes 52
  281.9 45.6 %all-to-all-start.3 = ((f32[8,24,2304]{2,1,0:T(8,128)}), f32[8,24,2304]{2,1,0:T(8,128)S(1)}, u32[]{:S(2)}, u32[]{:S(2)}) async-start(f32[8,24,2304]{2,1,0:T(8,128)} %bitcast.14), calls=%async_computation.3 | async-start | bytes 3538944 | tf_op jit(solution)/shard_map/all_to_all | solution.py:60
  327.4 84.7 %all-to-all-start.4 = ((f32[8,24,4608]{2,1,0:T(8,128)}), f32[8,24,4608]{2,1,0:T(8,128)}, u32[]{:S(2)}, u32[]{:S(2)}) async-start(f32[8,24,4608]{2,1,0:T(8,128)} %bitcast.138), calls=%async_computation.4 | async-start | bytes 7077888 | tf_op jit(solution)/shard_map/all_to_all | solution.py:60
  333.5 91.3 %collective-permute-start.4 = (f32[3456,128]{1,0:T(8,128)}, f32[3456,128]{1,0:T(8,128)}, u32[]{:S(2)}, u32[]{:S(2)}) collective-permute-start(f32[3456,128]{1,0:T(8,128)} %reshape.216), channel_id=1, source_target_pairs={{0,24},{8,16},{16,8},{24,0},{1,25},{9,17},{17,9},{25,1},{2,26},{10... | collective-permute-start | bytes 5308424 | tf_op jit(solution)/shard_map/ppermute | solution.py:13
  412.1 84.9 %all-to-all-start.5 = ((f32[8,24,4608]{2,1,0:T(8,128)}), f32[8,24,4608]{2,1,0:T(8,128)}, u32[]{:S(2)}, u32[]{:S(2)}) async-start(f32[8,24,4608]{2,1,0:T(8,128)} %bitcast.137), calls=%async_computation.5 | async-start | bytes 7077888 | tf_op jit(solution)/shard_map/all_to_all | solution.py:60
  435.1 28.8 %collective-permute-start.5 = (f32[2304,128]{1,0:T(8,128)}, f32[2304,128]{1,0:T(8,128)}, u32[]{:S(2)}, u32[]{:S(2)}) collective-permute-start(f32[2304,128]{1,0:T(8,128)} %reshape.218), channel_id=1, source_target_pairs={{0,8},{8,24},{16,0},{24,16},{1,9},{9,25},{17,1},{25,17},{2,10},{10... | collective-permute-start | bytes 3538952 | tf_op jit(solution)/shard_map/ppermute | solution.py:13
  463.9 53.3 %collective-permute-start.6 = (f32[4608,128]{1,0:T(8,128)}, f32[4608,128]{1,0:T(8,128)}, u32[]{:S(2)}, u32[]{:S(2)}) collective-permute-start(f32[4608,128]{1,0:T(8,128)} %reshape.226), channel_id=1, source_target_pairs={{0,8},{8,24},{16,0},{24,16},{1,9},{9,25},{17,1},{25,17},{2,10},{10... | collective-permute-start | bytes 7077896 | tf_op jit(solution)/shard_map/ppermute | solution.py:13
  474.2 7.3 %copy-start.2 = (f32[16,192,192]{2,1,0:T(8,128)S(1)}, f32[16,192,192]{2,1,0:T(8,128)}, u32[]{:S(2)}) copy-start(f32[16,192,192]{2,1,0:T(8,128)} %get-tuple-element.49) | copy-start | bytes 7077892
  (4 other events, 11.0 us)
